TPU v7x, 32 devices: a whole 2x2x4 slice. The times are simulated.
32 devices in a mesh: depth: 2 (over core), row: 4 (over y, x), col: 4 (over z).
Axes of the slice: x: 2, y: 2, z: 4, core: 2. Of those that a mesh axis runs over, the one named last changes fastest.
Arguments:
- activations: bfloat16 [2048, 6144], P('depth', ('row', 'col')), may hold values from -1000 to 1000
- norm_gain: bfloat16 [6144], P(('row', 'col')), may hold values from 0.099609375 to 1.8984375
- up_weight: bfloat16 [6144, 12288], P('row', 'col'), may hold values from -0.078125 to 0.078125
- down_weight: bfloat16 [12288, 6144], P('col', 'row'), may hold values from -0.0546875 to 0.0546875
- upstream: bfloat16 [2048, 6144], P('depth', ('row', 'col')), may hold values from -6 to 6
Outputs:
- branch: bfloat16 [2048, 6144], P('depth', ('row', 'col'))
- grad_input: bfloat16 [2048, 6144], P('depth', ('row', 'col'))
- grad_up: float32 [6144, 12288], P('row', ('col', 'depth'))
- grad_down: float32 [12288, 6144], P('col', ('row', 'depth'))
- grad_gain: float32 [6144], P(('row', 'col', 'depth'))
All inputs are finite; a program needn't handle non-finite values.
Results may differ from a plain program's by a relative error of at most 0.018.
Values may be sent and summed in bfloat16 or wider, within the bound.
A program may use at most 192 MiB of HBM per device.

v0:
```python
import jax
import jax.numpy as jnp
from jax import lax
from jax.sharding import PartitionSpec as P

D = 6144


EPSILON = 1e-06
INV_ROOT2 = 0.7071067811865476
INV_ROOT_TAU = 0.3989422804014327


def gelu_value(values):
    return 0.5 * values * (1.0 + jax.scipy.special.erf(values * INV_ROOT2))


def gelu_slope(values):
    return 0.5 * (
        1.0 + jax.scipy.special.erf(values * INV_ROOT2)
    ) + values * INV_ROOT_TAU * jnp.exp(-0.5 * values * values)


def inner_rows(left, right):
    return lax.dot_general(
        left, right, (((0,), (0,)), ((), ())), preferred_element_type=jnp.float32
    )


def inner_cols(left, right):
    return lax.dot_general(
        left, right, (((1,), (1,)), ((), ())), preferred_element_type=jnp.float32
    )


def body(activations, norm_gain, up_weight, down_weight, upstream):
    shard_width = activations.shape[1]
    gain_local = norm_gain.astype(jnp.float32)
    local = activations.astype(jnp.float32)
    first, second = lax.psum(
        (jnp.sum(local, axis=1), jnp.sum(local * local, axis=1)), ("row", "col")
    )
    centre = (first / D)[:, None]
    spread = lax.rsqrt(second[:, None] / D - centre * centre + EPSILON)
    whitened = (local - centre) * spread
    normed = lax.all_gather((whitened * gain_local).astype(jnp.bfloat16), "col", axis=1, tiled=True)
    partial_up = jnp.dot(normed, up_weight, preferred_element_type=jnp.float32)
    pre_act = lax.psum_scatter(
        partial_up.astype(jnp.bfloat16), "row", scatter_dimension=1, tiled=True
    ).astype(jnp.float32)
    activated = lax.all_gather(gelu_value(pre_act).astype(jnp.bfloat16), "row", axis=1, tiled=True)
    partial_down = jnp.dot(activated, down_weight, preferred_element_type=jnp.float32)
    branch = lax.psum_scatter(
        partial_down.astype(jnp.bfloat16), "col", scatter_dimension=1, tiled=True
    )
    grad_rows = lax.all_gather(upstream, "col", axis=1, tiled=True)
    grad_down_local = inner_rows(activated, grad_rows)
    partial_hidden = inner_cols(grad_rows, down_weight)
    grad_pre = lax.psum_scatter(
        partial_hidden.astype(jnp.bfloat16), "row", scatter_dimension=1, tiled=True
    ).astype(jnp.float32)
    gated = lax.all_gather(
        (grad_pre * gelu_slope(pre_act)).astype(jnp.bfloat16), "row", axis=1, tiled=True
    )
    grad_up_local = inner_rows(normed, gated)
    partial_normed = inner_cols(gated, up_weight)
    grad_normed = lax.psum_scatter(
        partial_normed.astype(jnp.bfloat16), "col", scatter_dimension=1, tiled=True
    ).astype(jnp.float32)
    scaled = grad_normed * gain_local
    total_grad, total_cross = lax.psum(
        (jnp.sum(scaled, axis=1), jnp.sum(scaled * whitened, axis=1)), ("row", "col")
    )
    mean_grad = (total_grad / D)[:, None]
    mean_cross = (total_cross / D)[:, None]
    grad_input = (spread * (scaled - mean_grad - whitened * mean_cross)).astype(jnp.bfloat16)
    gain_part = jnp.sum(grad_normed * whitened, axis=0).reshape(1, shard_width)
    grad_up, grad_down, gain_total = (
        lax.psum_scatter(
            grad_up_local.astype(jnp.bfloat16), "depth", scatter_dimension=1, tiled=True
        ).astype(jnp.float32),
        lax.psum_scatter(
            grad_down_local.astype(jnp.bfloat16), "depth", scatter_dimension=1, tiled=True
        ).astype(jnp.float32),
        lax.psum_scatter(
            gain_part.astype(jnp.bfloat16), "depth", scatter_dimension=1, tiled=True
        ).astype(jnp.float32),
    )
    return (branch, grad_input, grad_up, grad_down, gain_total.reshape(-1))


def solution(mesh):
    in_specs = (
        P("depth", ("row", "col")),
        P(("row", "col")),
        P("row", "col"),
        P("col", "row"),
        P("depth", ("row", "col")),
    )
    out_specs = (
        P("depth", ("row", "col")),
        P("depth", ("row", "col")),
        P("row", ("col", "depth")),
        P("col", ("row", "depth")),
        P(("row", "col", "depth")),
    )
    return jax.shard_map(body, mesh=mesh, in_specs=in_specs, out_specs=out_specs, check_vma=False)
```

profile of v0, /device:TPU:0, one launch (start us, length us, event | category | flops | bytes accessed | tf_op | source)
XLA Modules:
  0.0 667.9 jit_solution(10043201904914717054)
XLA Ops:
  9.4 44.5 %all-reduce.1 = (f32[1024]{0:T(1024)S(1)}, f32[1024]{0:T(1024)S(1)}) all-reduce(f32[1024]{0:T(1024)S(1)} %get-tuple-element.9, f32[1024]{0:T(1024)S(1)} %get-tuple-element.8), channel_id=1, replica_groups=mesh['depth'=2,'row'=4,'col'=4] {'row','col'}, use_global_device_ids=true, to_apply=%region_3.0 | all-reduce | flops 2048 | bytes 16384 | tf_op jit(solution)/shard_map/psum | solution.py:40
  53.9 2.4 fusion.20
  57.1 58.9 %all-gather.5.cloned.1.call-done = bf16[1024,1536]{1,0:T(8,128)(2,1)} async-done(((bf16[1024,384]{1,0:T(8,128)(2,1)}), bf16[1024,1536]{1,0:T(8,128)(2,1)}) %all-gather.5.cloned.1.call-update) | async-done | bytes 3145744 | tf_op jit(solution)/shard_map/all_gather | solution.py:46
  116.0 15.1 %convolution_convert_fusion.3 = bf16[1024,3072]{1,0:T(8,128)(2,1)} fusion(bf16[1024,1536]{1,0:T(8,128)(2,1)} %all-gather.5.cloned.1.call-done, bf16[1536,3072]{1,0:T(8,128)(2,1)} %param.7), kind=kOutput, calls=%fused_computation.8 | convolution fusion | flops 9666822144 | bytes 18874368 | tf_op jit(solution)/shard_map/dot_general | solution.py:47
  131.1 48.4 %all-gather.9.cloned.1.call-done = bf16[1024,1536]{1,0:T(8,128)(2,1)} async-done(((bf16[1024,384]{1,0:T(8,128)(2,1)}), bf16[1024,1536]{1,0:T(8,128)(2,1)}) %all-gather.9.cloned.1.call-update) | async-done | bytes 3145744 | tf_op jit(solution)/shard_map/all_gather | solution.py:56
  179.5 15.1 %convolution_convert_fusion.2 = bf16[1024,3072]{1,0:T(8,128)(2,1)} fusion(bf16[1024,1536]{1,0:T(8,128)(2,1)} %all-gather.9.cloned.1.call-done, bf16[3072,1536]{1,0:T(8,128)(2,1)} %param.8), kind=kOutput, calls=%fused_computation.7 | convolution fusion | flops 9666822144 | bytes 18874368 | tf_op jit(solution)/shard_map/dot_general | solution.py:31
  194.7 57.2 %reduce-scatter.14.cloned.1.call-done = bf16[1024,768]{1,0:T(8,128)(2,1)} async-done(((bf16[1024,3072]{1,0:T(8,128)(2,1)}), bf16[1024,768]{1,0:T(8,128)(2,1)}) %reduce-scatter.14.cloned.1.call-update) | async-done | bytes 1572880 | tf_op jit(solution)/shard_map/reduce_scatter | solution.py:48
  251.9 73.6 %reduce-scatter.16.cloned.1.call-done = bf16[1024,768]{1,0:T(8,128)(2,1)} async-done(((bf16[1024,3072]{1,0:T(8,128)(2,1)}), bf16[1024,768]{1,0:T(8,128)(2,1)}) %reduce-scatter.16.cloned.1.call-update) | async-done | bytes 1572880 | tf_op jit(solution)/shard_map/reduce_scatter | solution.py:59
  325.5 4.3 fusion.7
  330.5 69.7 %all-gather.11.cloned.1.call-done = bf16[1024,3072]{1,0:T(8,128)(2,1)} async-done(((bf16[1024,768]{1,0:T(8,128)(2,1)}), bf16[1024,3072]{1,0:T(8,128)(2,1)}) %all-gather.11.cloned.1.call-update) | async-done | bytes 6291472 | tf_op jit(solution)/shard_map/all_gather | solution.py:62
  400.2 14.1 %convolution_convert_fusion.4 = bf16[1024,1536]{1,0:T(8,128)(2,1)S(1)} fusion(bf16[1024,3072]{1,0:T(8,128)(2,1)} %all-gather.11.cloned.1.call-done, bf16[1536,3072]{1,0:T(8,128)(2,1)} %param.7), kind=kOutput, calls=%fused_computation.9 | convolution fusion | flops 9665249280 | bytes 18874368 | tf_op jit(solution)/shard_map/dot_general | solution.py:31
  414.3 2.9 copy.12
  417.4 55.2 %all-gather.7.cloned.1.call-done = bf16[1024,3072]{1,0:T(8,128)(2,1)} async-done(((bf16[1024,768]{1,0:T(8,128)(2,1)}), bf16[1024,3072]{1,0:T(8,128)(2,1)}) %all-gather.7.cloned.1.call-update) | async-done | bytes 6291472 | tf_op jit(solution)/shard_map/all_gather | solution.py:51
  472.6 14.0 %convolution_convert_fusion.5 = bf16[1024,1536]{1,0:T(8,128)(2,1)S(1)} fusion(bf16[1024,3072]{1,0:T(8,128)(2,1)} %all-gather.7.cloned.1.call-done, bf16[3072,1536]{1,0:T(8,128)(2,1)} %param.8), kind=kOutput, calls=%fused_computation.10 | convolution fusion | flops 9665249280 | bytes 18874368 | tf_op jit(solution)/shard_map/dot_general | solution.py:52
  486.7 2.9 copy.10
  489.6 46.2 %reduce-scatter.24.cloned.1.call-done = bf16[384,1024]{1,0:T(8,128)(2,1)} async-done(((bf16[1536,1024]{1,0:T(8,128)(2,1)}), bf16[384,1024]{1,0:T(8,128)(2,1)}) %reduce-scatter.24.cloned.1.call-update) | async-done | bytes 786448
  539.1 15.3 %convolution_convert_fusion.1 = bf16[1536,3072]{1,0:T(8,128)(2,1)} fusion(bf16[1024,1536]{1,0:T(8,128)(2,1)} %all-gather.5.cloned.1.call-done, bf16[1024,3072]{1,0:T(8,128)(2,1)} %all-gather.11.cloned.1.call-done), kind=kOutput, calls=%fused_computation.1 | convolution fusion | flops 9668395008 | bytes 18874368 | tf_op jit(solution)/shard_map/dot_general | solution.py:25
  554.7 15.3 %convolution_convert_fusion = bf16[3072,1536]{1,0:T(8,128)(2,1)} fusion(bf16[1024,3072]{1,0:T(8,128)(2,1)} %all-gather.7.cloned.1.call-done, bf16[1024,1536]{1,0:T(8,128)(2,1)} %all-gather.9.cloned.1.call-done), kind=kOutput, calls=%fused_computation | convolution fusion | flops 9668395008 | bytes 18874368 | tf_op jit(solution)/shard_map/dot_general | solution.py:25
  570.1 28.9 %reduce-scatter.22.cloned.1.call-done = bf16[384,1024]{1,0:T(8,128)(2,1)} async-done(((bf16[1536,1024]{1,0:T(8,128)(2,1)}), bf16[384,1024]{1,0:T(8,128)(2,1)}) %reduce-scatter.22.cloned.1.call-update) | async-done | bytes 786448
  599.0 2.3 copy.11
  601.3 41.5 %all-reduce = (f32[1024]{0:T(1024)S(1)}, f32[1024]{0:T(1024)S(1)}) all-reduce(f32[1024]{0:T(1024)S(1)} %get-tuple-element.6, f32[1024]{0:T(1024)S(1)} %get-tuple-element.7), channel_id=1, replica_groups=mesh['depth'=2,'row'=4,'col'=4] {'row','col'}, use_global_device_ids=true, to_apply=%region_11.0 | all-reduce | flops 2048 | bytes 16384 | tf_op jit(solution)/shard_map/psum | solution.py:71
  642.8 1.6 fusion.14
  645.9 8.6 %convert_element_type.80 = f32[1536,1536]{1,0:T(8,128)} convert(bf16[1536,1536]{1,0:T(8,128)(2,1)} %reduce-scatter.18.cloned.1.call-done) | non-fusion elementwise | flops 2359296 | bytes 14155776 | tf_op jit(solution)/shard_map/convert_element_type | solution.py:81
  654.5 6.8 %convert_element_type.82 = f32[3072,768]{1,0:T(8,128)} convert(bf16[3072,768]{1,0:T(8,128)(2,1)} %reduce-scatter.20.cloned.1.call-done) | non-fusion elementwise | flops 2359296 | bytes 14155776 | tf_op jit(solution)/shard_map/convert_element_type | solution.py:84
  (36 shorter events, 9.1 us)
Async XLA Ops:
  7.2 108.8 %all-gather.5.cloned.1.call-start = ((), (), s32[]{:S(2)}) async-start(), calls=%async_computation.7 | async-start | bytes 3932160 | tf_op jit(solution)/shard_map/all_gather | solution.py:46
  56.3 123.2 %all-gather.9.cloned.1.call-start = ((), (), s32[]{:S(2)}) async-start(), calls=%async_computation.10 | async-start | bytes 3932160 | tf_op jit(solution)/shard_map/all_gather | solution.py:56
  57.1 194.9 %reduce-scatter.14.cloned.1.call-start = ((), (), s32[]{:S(2)}) async-start(), calls=%async_computation.8 | async-start | bytes 7864320 | tf_op jit(solution)/shard_map/reduce_scatter | solution.py:48
  131.1 194.5 %reduce-scatter.16.cloned.1.call-start = ((), (), s32[]{:S(2)}) async-start(), calls=%async_computation.11 | async-start | bytes 7864320 | tf_op jit(solution)/shard_map/reduce_scatter | solution.py:59
  194.7 205.5 %all-gather.11.cloned.1.call-start = ((), (), s32[]{:S(2)}) async-start(), calls=%async_computation.12 | async-start | bytes 7864320 | tf_op jit(solution)/shard_map/all_gather | solution.py:62
  329.8 142.8 %all-gather.7.cloned.1.call-start = ((), (), s32[]{:S(2)}) async-start(), calls=%async_computation.9 | async-start | bytes 7864320 | tf_op jit(solution)/shard_map/all_gather | solution.py:51
  330.4 205.4 %reduce-scatter.24.cloned.1.call-start = ((), (), s32[]{:S(2)}) async-start(), calls=%async_computation.16 | async-start | bytes 3932160
  417.2 181.8 %reduce-scatter.22.cloned.1.call-start = ((), (), s32[]{:S(2)}) async-start(), calls=%async_computation.15 | async-start | bytes 3932160
  489.5 47.8 %copy-start = (bf16[1024,384]{1,0:T(8,128)(2,1)S(1)}, bf16[1024,384]{1,0:T(8,128)(2,1)}, u32[]{:S(2)}) copy-start(bf16[1024,384]{1,0:T(8,128)(2,1)} %param.5) | copy-start | bytes 2359300
  489.6 154.9 %reduce-scatter.26.cloned.1.call-start = ((), (), s32[]{:S(2)}) async-start(), calls=%async_computation.17 | async-start | bytes 147456
  539.1 106.9 %reduce-scatter.18.cloned.1.call-start = ((), (), s32[]{:S(2)}) async-start(), calls=%async_computation.13 | async-start | bytes 14155776 | tf_op jit(solution)/shard_map/reduce_scatter | solution.py:79
  554.4 100.1 %reduce-scatter.20.cloned.1.call-start = ((), (), s32[]{:S(2)}) async-start(), calls=%async_computation.14 | async-start | bytes 14155776 | tf_op jit(solution)/shard_map/reduce_scatter | solution.py:82
Sparse Core Ops, SparseCore 0:
  56.4 59.5 all-gather.4
  117.5 61.9 all-gather.8
  183.1 68.8 reduce-scatter.13
  255.3 70.1 reduce-scatter.15
  330.0 70.1 all-gather.10
  402.4 70.1 all-gather.6
  475.5 60.2 reduce-scatter.23
  538.7 60.2 reduce-scatter.21
  601.2 7.4 reduce-scatter.25
  611.5 18.9 reduce-scatter.17
  632.8 19.0 reduce-scatter.19
where the time goes:
time: 668 us
  waiting for transfers between devices  440 us (66%)
  matrix products  89 us (13%)
  blocking collectives  86 us (13%)
  other arithmetic  27.7 us (4%)
  between operations  13.9 us (2%)
  local copies, waits for them, and re-layouts  10.9 us (2%)
    unnamed x14, waiting for transfers between devices  76.5 us
    reduce_scatter x1, waiting for transfers between devices, body(): lax.psum_scatter(partial_hidden.astype(jnp.bfloat16), 'row', scatter_dime...  73.6 us
    all_gather x1, waiting for transfers between devices, body(): lax.all_gather((grad_pre * gelu_slope(pre_act)).astype(jnp.bfloat16), 'ro...  69.7 us
    all_gather x1, waiting for transfers between devices, body(): lax.all_gather((whitened * gain_local).astype(jnp.bfloat16), 'col', axis=...  58.9 us
    reduce_scatter x1, waiting for transfers between devices, body(): lax.psum_scatter(partial_up.astype(jnp.bfloat16), 'row', scatter_dimensio...  57.2 us
    all_gather x1, waiting for transfers between devices, body(): lax.all_gather(gelu_value(pre_act).astype(jnp.bfloat16), 'row', axis=1, t...  55.2 us
    all_gather x1, waiting for transfers between devices, body(): grad_rows = lax.all_gather(upstream, 'col', axis=1, tiled=True)  48.4 us
    psum x1, blocking collectives, body(): lax.psum((jnp.sum(local, axis=1), jnp.sum(local * local, axis=1)), ('row'...  44.5 us
  transfers between devices with their start and end apart: 11, of which 8 were waited for; matrix products, arithmetic and copies ran while one was open for 17% of the time, Pallas kernels for 0%

commit v1 on v0

--- a/solution.py
+++ b/solution.py
@@ -4,6 +4,8 @@
 from jax.sharding import PartitionSpec as P
 
 D = 6144
+CHUNKS = 2
+LAG = 2
 
 
 EPSILON = 1e-06
@@ -33,7 +35,7 @@
     )
 
 
-def body(activations, norm_gain, up_weight, down_weight, upstream):
+def plain_body(activations, norm_gain, up_weight, down_weight, upstream):
     shard_width = activations.shape[1]
     gain_local = norm_gain.astype(jnp.float32)
     local = activations.astype(jnp.float32)
@@ -89,6 +91,201 @@
     return (branch, grad_input, grad_up, grad_down, gain_total.reshape(-1))
 
 
+def take_block(values, axis, index, width):
+    return lax.dynamic_slice_in_dim(values, index * width, width, axis)
+
+
+def reorder(values, axis, order, width):
+    return jnp.concatenate([take_block(values, axis, index, width) for index in order], axis=axis)
+
+
+RING_UP = [(0, 1), (1, 2), (2, 3), (3, 0)]
+RING_DOWN = [(0, 3), (1, 0), (2, 1), (3, 2)]
+RING_TWO = [(0, 2), (1, 3), (2, 0), (3, 1)]
+
+
+def over_x(values):
+    return lax.ppermute(values, "row", [(0, 1), (1, 0), (2, 3), (3, 2)])
+
+
+def over_y(values):
+    return lax.ppermute(values, "row", [(0, 2), (2, 0), (1, 3), (3, 1)])
+
+
+def over_core(values):
+    return lax.ppermute(values, "depth", [(0, 1), (1, 0)])
+
+
+def total_over_slice(values):
+    values = values + over_x(values)
+    values = values + over_y(values)
+    return (
+        values
+        + lax.ppermute(values, "col", RING_UP)
+        + lax.ppermute(values, "col", RING_DOWN)
+        + lax.ppermute(values, "col", RING_TWO)
+    )
+
+
+def gather_col(values):
+    pieces = [values]
+    for _ in range(3):
+        pieces.append(lax.ppermute(pieces[-1], "col", RING_DOWN))
+    return pieces
+
+
+def scatter_col(partial):
+    width = partial.shape[1] // 4
+    block = lambda j: partial[:, j * width:(j + 1) * width]
+    moving = block(3)
+    for j in (2, 1, 0):
+        moving = block(j).astype(jnp.float32) + lax.ppermute(moving, "col", RING_UP).astype(jnp.float32)
+        if j:
+            moving = moving.astype(jnp.bfloat16)
+    return moving
+
+
+def gather_row(values):
+    half = values.shape[0] // 2
+    top, low = values[:half], values[half:]
+    top_x, low_y = over_x(top), over_y(low)
+    top_y, low_x = over_y(top), over_x(low)
+    return jnp.concatenate(
+        [
+            jnp.concatenate([top, top_x, top_y, over_y(top_x)], axis=1),
+            jnp.concatenate([low, low_x, low_y, over_x(low_y)], axis=1),
+        ],
+        axis=0,
+    )
+
+
+def scatter_row(partial):
+    half, width = partial.shape[0] // 2, partial.shape[1] // 4
+    top = lambda j: partial[:half, j * width:(j + 1) * width]
+    low = lambda j: partial[half:, j * width:(j + 1) * width]
+    wide = lambda values: values.astype(jnp.float32)
+    top_far, low_far = over_x(top(3)), over_y(low(3))
+    top_near, low_near = over_x(top(1)), over_y(low(2))
+    top_last = over_y((wide(top(2)) + wide(top_far)).astype(jnp.bfloat16))
+    low_last = over_x((wide(low(1)) + wide(low_far)).astype(jnp.bfloat16))
+    return jnp.concatenate(
+        [
+            wide(top(0)) + wide(top_near) + wide(top_last),
+            wide(low(0)) + wide(low_near) + wide(low_last),
+        ],
+        axis=0,
+    )
+
+
+def after(values, earlier):
+    return lax.optimization_barrier((values, earlier))[0]
+
+
+def body(activations, norm_gain, up_weight, down_weight, upstream):
+    tokens, shard = activations.shape
+    row, col, core = lax.axis_index("row"), lax.axis_index("col"), lax.axis_index("depth")
+    hidden = up_weight.shape[1] // 4
+    turned = [lax.rem(col + j, 4) for j in range(4)]
+    turned_back = [lax.rem(j - col + 4, 4) for j in range(4)]
+    flipped = [row ^ j for j in range(4)]
+
+    local = activations.astype(jnp.float32)
+    sums = total_over_slice(
+        jnp.stack([jnp.sum(local, axis=1), jnp.sum(local * local, axis=1)], axis=0)
+    )
+    gain_local = norm_gain.astype(jnp.float32).reshape(1, shard)
+    gain_block = jnp.concatenate(gather_col(gain_local), axis=1)
+    centre = (sums[0] / D)[:, None]
+    spread = lax.rsqrt(sums[1][:, None] / D - centre * centre + EPSILON)
+
+    up = reorder(reorder(up_weight, 0, turned, shard), 1, flipped, hidden)
+    down = reorder(reorder(down_weight, 1, turned, shard), 0, flipped, hidden)
+
+    size = tokens // CHUNKS
+    parts = [slice(k * size, (k + 1) * size) for k in range(CHUNKS)]
+    behind = None
+    grad_rows, raw = [], []
+    for part in parts:
+        for source, store in ((upstream, grad_rows), (activations, raw)):
+            piece = source[part]
+            if behind is not None:
+                piece = after(piece, behind)
+            pieces = gather_col(piece)
+            behind = pieces[LAG]
+            store.append(jnp.concatenate(pieces, axis=1))
+
+    whitened, normed, activated, gated, branch, grad_normed, sums_back = ([] for _ in range(7))
+    for k, part in enumerate(parts):
+        grad_pre = scatter_row(inner_cols(grad_rows[k], down).astype(jnp.bfloat16))
+        whitened.append((raw[k].astype(jnp.float32) - centre[part]) * spread[part])
+        normed.append((whitened[k] * gain_block).astype(jnp.bfloat16))
+        pre_act = scatter_row(
+            jnp.dot(normed[k], up, preferred_element_type=jnp.float32).astype(jnp.bfloat16)
+        )
+        activated.append(gather_row(gelu_value(pre_act).astype(jnp.bfloat16)))
+        gated.append(gather_row((grad_pre * gelu_slope(pre_act)).astype(jnp.bfloat16)))
+        branch.append(
+            scatter_col(
+                jnp.dot(activated[k], down, preferred_element_type=jnp.float32).astype(jnp.bfloat16)
+            ).astype(jnp.bfloat16)
+        )
+        partial = inner_cols(gated[k], up).astype(jnp.bfloat16)
+        wide = partial.astype(jnp.float32) * gain_block
+        sums_back.append(
+            total_over_slice(
+                jnp.stack([jnp.sum(wide, axis=1), jnp.sum(wide * whitened[k], axis=1)], axis=0)
+            )
+        )
+        grad_normed.append(scatter_col(partial))
+
+    def over_tokens(blocks, axis_order, width):
+        return jnp.concatenate([reorder(block, 1, axis_order, width) for block in blocks], axis=0)
+
+    def split(order):
+        keep = [jnp.where(core == 0, order[b], order[2 + b]) for b in range(2)]
+        send = [jnp.where(core == 0, order[2 + b], order[b]) for b in range(2)]
+        return keep, send
+
+    hidden_keep, hidden_send = split(flipped)
+    width_keep, width_send = split(turned_back)
+
+    whole_activated = over_tokens(activated, flipped, hidden)
+    down_send = inner_rows(whole_activated, over_tokens(grad_rows, width_send, shard))
+    down_got = over_core(down_send.astype(jnp.bfloat16))
+    grad_down = inner_rows(
+        whole_activated, over_tokens(grad_rows, width_keep, shard)
+    ) + down_got.astype(jnp.float32)
+
+    whole_normed = over_tokens(normed, turned_back, shard)
+    up_send = inner_rows(whole_normed, over_tokens(gated, hidden_send, hidden))
+    up_got = over_core(up_send.astype(jnp.bfloat16))
+    grad_up = inner_rows(
+        whole_normed, over_tokens(gated, hidden_keep, hidden)
+    ) + up_got.astype(jnp.float32)
+
+    grad_input, gain_part = [], 0.0
+    for k, part in enumerate(parts):
+        white = (local[part] - centre[part]) * spread[part]
+        scaled = grad_normed[k] * gain_local
+        mean_grad = (sums_back[k][0] / D)[:, None]
+        mean_cross = (sums_back[k][1] / D)[:, None]
+        grad_input.append(
+            (spread[part] * (scaled - mean_grad - white * mean_cross)).astype(jnp.bfloat16)
+        )
+        gain_part = gain_part + jnp.sum(grad_normed[k] * white, axis=0, keepdims=True)
+    half = shard // 2
+    gain_total = take_block(gain_part, 1, core, half) + over_core(
+        take_block(gain_part, 1, 1 - core, half)
+    )
+    return (
+        jnp.concatenate(branch, axis=0),
+        jnp.concatenate(grad_input, axis=0),
+        grad_up,
+        grad_down,
+        gain_total.reshape(-1),
+    )
+
+
 def solution(mesh):
     in_specs = (
         P("depth", ("row", "col")),
@@ -104,4 +301,5 @@
         P("col", ("row", "depth")),
         P(("row", "col", "depth")),
     )
-    return jax.shard_map(body, mesh=mesh, in_specs=in_specs, out_specs=out_specs, check_vma=False)
+    paired = mesh.shape["row"] == 4 and mesh.shape["col"] == 4 and mesh.shape["depth"] == 2
+    return jax.shard_map(body if paired else plain_body, mesh=mesh, in_specs=in_specs, out_specs=out_specs, check_vma=False)

time: 668 us -> 627 us (0.939); the launches traced: 668 us -> 618 us
  waiting for transfers between devices: 440 us -> 193 us
  starting transfers between devices: 0.85 us -> 109 us
  matrix products: 89 us -> 193 us
  blocking collectives: 86 us -> 0 us
  local copies, waits for them, and re-layouts: 10.9 us -> 52 us
  other arithmetic: 27.7 us -> 68.4 us
  between operations: 13.9 us -> 2.09 us
    all_gather x4 -> x0, waiting for transfers between devices: 232 us -> none  [the longest x1 69.7 us: body(): lax.all_gather((grad_pre * gelu_slope(pre_act)).astype(jnp.bfloat16), 'ro...]
    ppermute x0 -> x93, waiting for transfers between devices: none -> 193 us  [the longest x12 83.4 us: scatter_col(): lax.ppermute(moving, 'col', RING_UP).astype(jnp.float32)]
    reduce_scatter x4 -> x0, waiting for transfers between devices: 131 us -> none  [the longest x1 73.6 us: body(): lax.psum_scatter(partial_hidden.astype(jnp.bfloat16), 'row', scatter_dime...]
    ppermute x0 -> x93, starting transfers between devices: none -> 109 us  [the longest x15 38.7 us: gather_col(): pieces.append(lax.ppermute(pieces[-1], 'col', RING_DOWN))]
    psum x2 -> x0, blocking collectives: 86 us -> none  [the longest x1 44.5 us: body(): lax.psum((jnp.sum(local, axis=1), jnp.sum(local * local, axis=1)), ('row'...]
    dot_general x2 -> x4, matrix products: 30.6 us -> 111 us  [inner_rows(): lax.dot_general(left, right, (((0,), (0,)), ((), ())), preferred_element_...]
    unnamed x14 -> x0, waiting for transfers between devices: 76.5 us -> none
    concatenate x0 -> x10, other arithmetic: none -> 43.7 us  [the longest x4 29.4 us: gather_row(): jnp.concatenate([jnp.concatenate([top, top_x, top_y, over_y(top_x)], axis...]
  transfers between devices with their start and end apart: 11 -> 93, of which waited for: 8 -> 41; matrix products, arithmetic and copies ran while one was open for 17% -> 42% of each run, Pallas kernels for 0% -> 0%
where the time goes in v1:
time: 627 us; the launch traced here: 618 us
  waiting for transfers between devices  193 us (31%)
  matrix products  193 us (31%)
  starting transfers between devices  109 us (17%)
  other arithmetic  68.4 us (11%)
  local copies, waits for them, and re-layouts  52 us (8%)
    dot_general x4, matrix products, inner_rows(): lax.dot_general(left, right, (((0,), (0,)), ((), ())), preferred_element_...  111 us
    ppermute x12, waiting for transfers between devices, scatter_col(): lax.ppermute(moving, 'col', RING_UP).astype(jnp.float32)  83.4 us
    ppermute x27, waiting for transfers between devices, over_y(): return lax.ppermute(values, 'row', [(0, 2), (2, 0), (1, 3), (3, 1)])  47.1 us
    dot_general x4, matrix products, inner_cols(): lax.dot_general(left, right, (((1,), (1,)), ((), ())), preferred_element_...  43.9 us
    ppermute x15, starting transfers between devices, gather_col(): pieces.append(lax.ppermute(pieces[-1], 'col', RING_DOWN))  38.7 us
    dynamic_slice x12, local copies, waits for them, and re-layouts, take_block(): return lax.dynamic_slice_in_dim(values, index * width, width, axis)  34.1 us
    ppermute x15, waiting for transfers between devices, gather_col(): pieces.append(lax.ppermute(pieces[-1], 'col', RING_DOWN))  30.7 us
    ppermute x27, starting transfers between devices, over_x(): return lax.ppermute(values, 'row', [(0, 1), (1, 0), (2, 3), (3, 2)])  29.9 us
  transfers between devices with their start and end apart: 93, of which 41 were waited for; matrix products, arithmetic and copies ran while one was open for 42% of the time, Pallas kernels for 0%

profile of v1, /device:TPU:0, one launch (start us, length us, event | category | flops | bytes accessed | tf_op | source)
XLA Modules:
  0.0 617.7 jit_solution(14821472140245101097)
XLA Ops:
  11.8 7.8 %constant_dynamic-slice_fusion.39 = (bf16[3072,384]{1,0:T(8,128)(2,1)}, bf16[3072,384]{1,0:T(8,128)(2,1)}, bf16[3072,384]{1,0:T(8,128)(2,1)}, bf16[3072,384]{1,0:T(8,128)(2,1)}) fusion(bf16[3072,1536]{1,0:T(8,128)(2,1)} %param.8, s32[]{:T(128)S(6)} %select_n.119, s32[]{:T(128)S(6)} %select_n.120, s32[]{:T(128)S(6)} %select_n.122, s32[]{:T(128)S(6)} %select_n.121), kind=kLoop, calls=%fused_computation.162 | loop fusion | bytes 18874384 | tf_op jit(solution)/shard_map/dynamic_slice | solution.py:95
  26.3 10.0 %pad_maximum_fusion.2 = bf16[3072,1536]{1,0:T(8,128)(2,1)} fusion(bf16[3072,384]{1,0:T(8,128)(2,1)} %get-tuple-element.27, bf16[3072,384]{1,0:T(8,128)(2,1)} %get-tuple-element.28, bf16[3072,384]{1,0:T(8,128)(2,1)} %get-tuple-element.26, bf16[3072,384]{1,0:T(8,128)(2,1)} %get-tuple-element.25), kind=kLoop, calls=%fused_computation.2 | loop fusion | flops 37748736 | bytes 18874368 | tf_op jit(solution)/shard_map/concatenate | solution.py:99
  77.0 10.4 %convolution_convert_fusion.3 = bf16[512,3072]{1,0:T(8,128)(2,1)S(1)} fusion(bf16[512,384]{1,0:T(8,128)(2,1)} %collective-permute-done.48, bf16[512,384]{1,0:T(8,128)(2,1)} %collective-permute-done.1, bf16[512,384]{1,0:T(8,128)(2,1)} %collective-permute-done, bf16[512,384]{1,0:T(8,128)(2,1)} %copy-done.12, bf16[768,1536]{1,0:T(8,128)(2,1)} %get-tuple-element.22, ...), kind=kOutput, calls=%fused_computation.10 | convolution fusion | flops 4877451264 | bytes 14155776 | tf_op jit(solution)/shard_map/dot_general | solution.py:33
  127.9 10.6 %convolution_convert_fusion.2 = bf16[512,3072]{1,0:T(8,128)(2,1)S(1)} fusion(bf16[512,1536]{1,0:T(8,128)(2,1)S(1)} %constant_dynamic-update-slice_fusion, bf16[768,1536]{1,0:T(8,128)(2,1)} %get-tuple-element.22, bf16[768,1536]{1,0:T(8,128)(2,1)} %get-tuple-element.23, bf16[768,1536]{1,0:T(8,128)(2,1)} %get-tuple-element.24, bf16[768,1536]{1,0:T(8,128)(2,1)} %copy-done.5), kind=kOutput, calls=%fused_computation.9 | convolution fusion | flops 4871159808 | bytes 14155776 | tf_op jit(solution)/shard_map/dot_general | solution.py:33
  160.9 8.6 %convolution_convert_fusion.4 = bf16[512,3072]{1,0:T(8,128)(2,1)S(1)} fusion(bf16[512,1536]{1,0:T(8,128)(2,1)S(1)} %get-tuple-element.112, bf16[1536,768]{1,0:T(8,128)(2,1)} %get-tuple-element.30, bf16[1536,768]{1,0:T(8,128)(2,1)} %get-tuple-element.31, bf16[1536,768]{1,0:T(8,128)(2,1)} %get-tuple-element.32, bf16[1536,768]{1,0:T(8,128)(2,1)S(1)} %copy-done.7), kind=kOutput, calls=%fused_computation.11 | convolution fusion | flops 4871159808 | bytes 14155776 | tf_op jit(solution)/shard_map/dot_general | solution.py:223
  171.4 9.1 %convolution_convert_fusion.5 = bf16[512,3072]{1,0:T(8,128)(2,1)S(1)} fusion(bf16[512,1536]{1,0:T(8,128)(2,1)S(1)} %get-tuple-element.111, bf16[1536,768]{1,0:T(8,128)(2,1)} %get-tuple-element.30, bf16[1536,768]{1,0:T(8,128)(2,1)} %get-tuple-element.31, bf16[1536,768]{1,0:T(8,128)(2,1)} %get-tuple-element.32, bf16[1536,768]{1,0:T(8,128)(2,1)} %get-tuple-element.29), kind=kOutput, calls=%fused_computation.12 | convolution fusion | flops 4871159808 | bytes 14155776 | tf_op jit(solution)/shard_map/dot_general | solution.py:223
  196.0 7.5 %collective-permute-done.33 = bf16[256,768]{1,0:T(8,128)(2,1)S(1)} collective-permute-done((bf16[256,768]{1,0:T(8,128)(2,1)S(1)}, bf16[256,768]{1,0:T(8,128)(2,1)S(1)}, u32[]{:S(2)}, u32[]{:S(2)}) %collective-permute-start.33) | collective-permute-done | bytes 393248 | tf_op jit(solution)/shard_map/ppermute | solution.py:108
  285.0 10.1 %convolution_convert_fusion.8 = bf16[512,1536]{1,0:T(8,128)(2,1)} fusion(bf16[256,768]{1,0:T(8,128)(2,1)} %copy-done.46, bf16[256,768]{1,0:T(8,128)(2,1)} %copy-done.42, bf16[256,768]{1,0:T(8,128)(2,1)} %copy-done.43, bf16[256,768]{1,0:T(8,128)(2,1)} %copy-done.15, bf16[256,768]{1,0:T(8,128)(2,1)} %copy-done.47, bf16[256,768]{1,0:T(8,128)(2,1)} %copy-done.45, ...), kind=kOutput, calls=%fused_computation.45 | convolution fusion | flops 4895539200 | bytes 14155776 | tf_op jit(solution)/shard_map/dot_general | solution.py:229
  323.0 13.4 %maximum_maximum_fusion.3 = bf16[512,3072]{1,0:T(8,128)(2,1)S(1)} fusion(bf16[256,768]{1,0:T(8,128)(2,1)S(1)} %collective-permute-done.60, bf16[256,768]{1,0:T(8,128)(2,1)} %collective-permute-done.59, bf16[256,768]{1,0:T(8,128)(2,1)S(1)} %collective-permute-done.58, bf16[256,768]{1,0:T(8,128)(2,1)} %get-tuple-element.100, ...), kind=kLoop, calls=%fused_computation.15 | loop fusion | flops 25165824 | bytes 6291456 | tf_op jit(solution)/shard_map/concatenate | solution.py:153
  338.8 7.4 %convolution_convert_fusion = bf16[1536,1536]{1,0:T(8,128)(2,1)} fusion(bf16[512,768]{1,0:T(8,128)(2,1)S(1)} %get-tuple-element.54, bf16[512,768]{1,0:T(8,128)(2,1)S(1)} %get-tuple-element.52, bf16[512,768]{1,0:T(8,128)(2,1)S(1)} %get-tuple-element.50, bf16[512,768]{1,0:T(8,128)(2,1)S(1)} %get-tuple-element.48, bf16[512,384]{1,0:T(8,128)(2,1)S(1)} %copy-done.61, ...), kind=kOutput, calls=%fused_computation.6 | convolution fusion | flops 4871946240 | bytes 11010048 | tf_op jit(solution)/shard_map/dot_general | solution.py:27
  346.2 11.0 %convolution_convert_fusion.6 = bf16[512,1536]{1,0:T(8,128)(2,1)} fusion(bf16[256,768]{1,0:T(8,128)(2,1)} %collective-permute-done.81, bf16[256,768]{1,0:T(8,128)(2,1)} %collective-permute-done.80, bf16[256,768]{1,0:T(8,128)(2,1)} %copy-done.48, bf16[256,768]{1,0:T(8,128)(2,1)} %copy-done.16, bf16[256,768]{1,0:T(8,128)(2,1)} %collective-permute-done.78, ...), kind=kOutput, calls=%fused_computation.43 | convolution fusion | flops 4895539200 | bytes 14155776 | tf_op jit(solution)/shard_map/dot_general | solution.py:33
  357.1 11.9 %fusion.18 = (f32[512]{0:T(512)S(1)}, f32[512]{0:T(512)S(1)}, f32[512]{0:T(512)}, f32[512]{0:T(512)}, bf16[512,1536]{1,0:T(8,128)(2,1)}) fusion(f32[1536]{0:T(1024)S(1)} %maximum_reduce_fusion, f32[512]{0:T(512)S(1)} %bitcast.36, f32[512]{0:T(512)S(1)} %bitcast.27, bf16[512,384]{1,0:T(8,128)(2,1)} %copy-done.38, ...), kind=kOutput, calls=%fused_computation.38 | convolution fusion | flops 4919130112 | bytes 18896896 | tf_op jit(solution)/shard_map/dot_general | solution.py:33
  387.2 44.8 %convolution_convert_fusion.1 = bf16[3072,768]{1,0:T(8,128)(2,1)} fusion(bf16[512,384]{1,0:T(8,128)(2,1)S(1)} %copy-done.67, bf16[512,384]{1,0:T(8,128)(2,1)S(1)} %copy-done.68, bf16[512,384]{1,0:T(8,128)(2,1)S(1)} %copy-done.58, bf16[512,384]{1,0:T(8,128)(2,1)S(1)} %copy-done.57, bf16[512,768]{1,0:T(8,128)(2,1)S(1)} %get-tuple-element.46, ...), kind=kOutput, calls=%fused_computation.8 | convolution fusion | flops 4890820608 | bytes 12582912 | tf_op jit(solution)/shard_map/dot_general | solution.py:27
  432.0 10.2 %convolution_convert_fusion.9 = bf16[512,1536]{1,0:T(8,128)(2,1)} fusion(bf16[256,768]{1,0:T(8,128)(2,1)} %collective-permute-done.24, bf16[256,768]{1,0:T(8,128)(2,1)} %collective-permute-done.23, bf16[256,768]{1,0:T(8,128)(2,1)} %collective-permute-done.22, bf16[256,768]{1,0:T(8,128)(2,1)} %get-tuple-element.104, ...), kind=kOutput, calls=%fused_computation.46 | convolution fusion | flops 4895539200 | bytes 14155776 | tf_op jit(solution)/shard_map/dot_general | solution.py:229
  467.2 16.8 %collective-permute-done.82 = bf16[512,384]{1,0:T(8,128)(2,1)S(1)} collective-permute-done((bf16[512,384]{1,0:T(8,128)(2,1)}, bf16[512,384]{1,0:T(8,128)(2,1)S(1)}, u32[]{:S(2)}, u32[]{:S(2)}) %collective-permute-start.82) | collective-permute-done | bytes 393248 | tf_op jit(solution)/shard_map/ppermute | solution.py:142
  485.1 7.3 %collective-permute-done.61 = bf16[512,384]{1,0:T(8,128)(2,1)S(1)} collective-permute-done((bf16[512,384]{1,0:T(8,128)(2,1)S(1)}, bf16[512,384]{1,0:T(8,128)(2,1)S(1)}, u32[]{:S(2)}, u32[]{:S(2)}) %collective-permute-start.61) | collective-permute-done | bytes 393248 | tf_op jit(solution)/shard_map/ppermute | solution.py:142
  494.3 15.0 %collective-permute-done.83 = bf16[512,384]{1,0:T(8,128)(2,1)S(1)} collective-permute-done((bf16[512,384]{1,0:T(8,128)(2,1)S(1)}, bf16[512,384]{1,0:T(8,128)(2,1)S(1)}, u32[]{:S(2)}, u32[]{:S(2)}) %collective-permute-start.83) | collective-permute-done | bytes 393248 | tf_op jit(solution)/shard_map/ppermute | solution.py:142
  509.4 8.3 %collective-permute-done.62 = bf16[512,384]{1,0:T(8,128)(2,1)S(1)} collective-permute-done((bf16[512,384]{1,0:T(8,128)(2,1)S(1)}, bf16[512,384]{1,0:T(8,128)(2,1)S(1)}, u32[]{:S(2)}, u32[]{:S(2)}) %collective-permute-start.62) | collective-permute-done | bytes 393248 | tf_op jit(solution)/shard_map/ppermute | solution.py:142
  518.6 7.5 %collective-permute-done.26 = bf16[512,384]{1,0:T(8,128)(2,1)S(1)} collective-permute-done((bf16[512,384]{1,0:T(8,128)(2,1)S(1)}, bf16[512,384]{1,0:T(8,128)(2,1)S(1)}, u32[]{:S(2)}, u32[]{:S(2)}) %collective-permute-start.26) | collective-permute-done | bytes 393248 | tf_op jit(solution)/shard_map/ppermute | solution.py:142
  526.3 8.3 %collective-permute-done.84 = bf16[512,384]{1,0:T(8,128)(2,1)S(1)} collective-permute-done((bf16[512,384]{1,0:T(8,128)(2,1)S(1)}, bf16[512,384]{1,0:T(8,128)(2,1)S(1)}, u32[]{:S(2)}, u32[]{:S(2)}) %collective-permute-start.84) | collective-permute-done | bytes 393248 | tf_op jit(solution)/shard_map/ppermute | solution.py:142
  534.6 8.4 %collective-permute-done.63 = bf16[512,384]{1,0:T(8,128)(2,1)S(1)} collective-permute-done((bf16[512,384]{1,0:T(8,128)(2,1)S(1)}, bf16[512,384]{1,0:T(8,128)(2,1)S(1)}, u32[]{:S(2)}, u32[]{:S(2)}) %collective-permute-start.63) | collective-permute-done | bytes 393248 | tf_op jit(solution)/shard_map/ppermute | solution.py:142
  544.1 7.3 %collective-permute-done.47 = bf16[512,384]{1,0:T(8,128)(2,1)S(1)} collective-permute-done((bf16[512,384]{1,0:T(8,128)(2,1)S(1)}, bf16[512,384]{1,0:T(8,128)(2,1)S(1)}, u32[]{:S(2)}, u32[]{:S(2)}) %collective-permute-start.47) | collective-permute-done | bytes 393248 | tf_op jit(solution)/shard_map/ppermute | solution.py:142
  558.7 11.4 %convert_add_fusion.1 = f32[1536,1536]{1,0:T(8,128)} fusion(bf16[1536,1536]{1,0:T(8,128)(2,1)} %collective-permute-done.90, bf16[512,768]{1,0:T(8,128)(2,1)S(1)} %copy-done.21, bf16[512,768]{1,0:T(8,128)(2,1)S(1)} %copy-done.20, bf16[512,768]{1,0:T(8,128)(2,1)S(1)} %copy-done.23, bf16[512,768]{1,0:T(8,128)(2,1)S(1)} %copy-done.22, ...), kind=kOutput, calls=%fused_computation.5 | convolution fusion | flops 4874305536 | bytes 20447232 | tf_op jit(solution)/shard_map/dot_general | solution.py:27
  570.2 47.3 %convert_add_fusion = f32[3072,768]{1,0:T(8,128)} fusion(bf16[3072,768]{1,0:T(8,128)(2,1)} %collective-permute-done.91, bf16[512,384]{1,0:T(8,128)(2,1)} %get-tuple-element.86, bf16[512,384]{1,0:T(8,128)(2,1)} %get-tuple-element.83, bf16[512,384]{1,0:T(8,128)(2,1)} %get-tuple-element.81, bf16[512,384]{1,0:T(8,128)(2,1)S(1)} %copy-done.56, ...), kind=kOutput, calls=%fused_computation.4 | convolution fusion | flops 4893179904 | bytes 22020096 | tf_op jit(solution)/shard_map/dot_general | solution.py:27
  (429 shorter events, 305.3 us)
Async XLA Ops:
  2.6 43.8 %collective-permute-start = (bf16[512,384]{1,0:T(8,128)(2,1)S(1)}, bf16[512,384]{1,0:T(8,128)(2,1)}, u32[]{:S(2)}, u32[]{:S(2)}) collective-permute-start(bf16[512,384]{1,0:T(8,128)(2,1)S(1)} %get-tuple-element.107), channel_id=1, source_target_pairs={{0,3},{1,0},{2,1},{3,2},{4,7},{5,4},{6,5},{7,6},{8,11},{9,8},{10,9... | collective-permute-start | bytes 1179656 | tf_op jit(solution)/shard_map/ppermute | solution.py:133
  8.3 36.0 %collective-permute-start.10 = (f32[1,384]{1,0:T(1,128)S(1)}, f32[1,384]{1,0:T(1,128)S(1)}, u32[]{:S(2)}, u32[]{:S(2)}) collective-permute-start(f32[1,384]{1,0:T(1,128)S(1)} %reshape.114), channel_id=1, source_target_pairs={{0,3},{1,0},{2,1},{3,2},{4,7},{5,4},{6,5},{7,6},{8,11},{9,8},{10,9... | collective-permute-start | bytes 4616 | tf_op jit(solution)/shard_map/ppermute | solution.py:133
  10.3 34.5 %collective-permute-start.5 = (f32[2,1024]{1,0:T(2,128)S(1)}, f32[2,1024]{1,0:T(2,128)S(1)}, u32[]{:S(2)}, u32[]{:S(2)}) collective-permute-start(f32[2,1024]{1,0:T(2,128)S(1)} %pad_maximum_fusion.11), channel_id=1, source_target_pairs={{0,4},{4,0},{8,12},{12,8},{1,5},{5,1},{9,13},{13,9},{2,6},{6,2},{1... | collective-permute-start | bytes 24584 | tf_op jit(solution)/shard_map/ppermute | solution.py:108
  93.9 26.4 %collective-permute-start.53 = (bf16[256,768]{1,0:T(8,128)(2,1)S(1)}, bf16[256,768]{1,0:T(8,128)(2,1)S(1)}, u32[]{:S(2)}, u32[]{:S(2)}) collective-permute-start(bf16[256,768]{1,0:T(8,128)(2,1)S(1)} %get-tuple-element.58), channel_id=1, source_target_pairs={{0,8},{8,0},{4,12},{12,4},{1,9},{9,1},{5,13},{13,5},{2,10},{10,2},... | collective-permute-start | bytes 1179656 | tf_op jit(solution)/shard_map/ppermute | solution.py:112
  94.4 50.3 %collective-permute-start.52 = (bf16[256,768]{1,0:T(8,128)(2,1)S(1)}, bf16[256,768]{1,0:T(8,128)(2,1)}, u32[]{:S(2)}, u32[]{:S(2)}) collective-permute-start(bf16[256,768]{1,0:T(8,128)(2,1)S(1)} %get-tuple-element.59), channel_id=1, source_target_pairs={{0,8},{8,0},{4,12},{12,4},{1,9},{9,1},{5,13},{13,5},{2,10},{10,2},... | collective-permute-start | bytes 1179656 | tf_op jit(solution)/shard_map/ppermute | solution.py:112
  109.0 46.7 %collective-permute-start.4 = (bf16[512,384]{1,0:T(8,128)(2,1)}, bf16[512,384]{1,0:T(8,128)(2,1)S(1)}, u32[]{:S(2)}, u32[]{:S(2)}) collective-permute-start(bf16[512,384]{1,0:T(8,128)(2,1)} %collective-permute-done.3), channel_id=1, source_target_pairs={{0,3},{1,0},{2,1},{3,2},{4,7},{5,4},{6,5},{7,6},{8,11},{9,8},{10,9... | collective-permute-start | bytes 1179656 | tf_op jit(solution)/shard_map/ppermute | solution.py:133
  146.0 38.9 %collective-permute-start.70 = (bf16[256,768]{1,0:T(8,128)(2,1)}, bf16[256,768]{1,0:T(8,128)(2,1)}, u32[]{:S(2)}, u32[]{:S(2)}) collective-permute-start(bf16[256,768]{1,0:T(8,128)(2,1)} %get-tuple-element.63), channel_id=1, source_target_pairs={{0,4},{4,0},{8,12},{12,8},{1,5},{5,1},{9,13},{13,9},{2,6},{6,2},{1... | collective-permute-start | bytes 1179656 | tf_op jit(solution)/shard_map/ppermute | solution.py:108
  147.3 39.0 %collective-permute-start.74 = (bf16[256,768]{1,0:T(8,128)(2,1)}, bf16[256,768]{1,0:T(8,128)(2,1)}, u32[]{:S(2)}, u32[]{:S(2)}) collective-permute-start(bf16[256,768]{1,0:T(8,128)(2,1)} %get-tuple-element.64), channel_id=1, source_target_pairs={{0,8},{8,0},{4,12},{12,4},{1,9},{9,1},{5,13},{13,5},{2,10},{10,2},... | collective-permute-start | bytes 1179656 | tf_op jit(solution)/shard_map/ppermute | solution.py:112
  154.4 53.1 %collective-permute-start.73 = (bf16[256,768]{1,0:T(8,128)(2,1)}, bf16[256,768]{1,0:T(8,128)(2,1)}, u32[]{:S(2)}, u32[]{:S(2)}) collective-permute-start(bf16[256,768]{1,0:T(8,128)(2,1)} %get-tuple-element.65), channel_id=1, source_target_pairs={{0,8},{8,0},{4,12},{12,4},{1,9},{9,1},{5,13},{13,5},{2,10},{10,2},... | collective-permute-start | bytes 1179656 | tf_op jit(solution)/shard_map/ppermute | solution.py:112
  155.7 31.1 %collective-permute-start.72 = (bf16[256,768]{1,0:T(8,128)(2,1)}, bf16[256,768]{1,0:T(8,128)(2,1)}, u32[]{:S(2)}, u32[]{:S(2)}) collective-permute-start(bf16[256,768]{1,0:T(8,128)(2,1)} %add_convert_fusion.3), channel_id=1, source_target_pairs={{0,8},{8,0},{4,12},{12,4},{1,9},{9,1},{5,13},{13,5},{2,10},{10,2},... | collective-permute-start | bytes 1179656 | tf_op jit(solution)/shard_map/ppermute | solution.py:112
  207.5 25.7 %collective-permute-start.36 = (bf16[256,768]{1,0:T(8,128)(2,1)S(1)}, bf16[256,768]{1,0:T(8,128)(2,1)S(1)}, u32[]{:S(2)}, u32[]{:S(2)}) collective-permute-start(bf16[256,768]{1,0:T(8,128)(2,1)S(1)} %copy-done.49), channel_id=1, source_target_pairs={{0,8},{8,0},{4,12},{12,4},{1,9},{9,1},{5,13},{13,5},{2,10},{10,2},... | collective-permute-start | bytes 1179656 | tf_op jit(solution)/shard_map/ppermute | solution.py:112
  250.0 25.4 %collective-permute-start.80 = (bf16[256,768]{1,0:T(8,128)(2,1)S(1)}, bf16[256,768]{1,0:T(8,128)(2,1)}, u32[]{:S(2)}, u32[]{:S(2)}) collective-permute-start(bf16[256,768]{1,0:T(8,128)(2,1)S(1)} %get-tuple-element.102), channel_id=1, source_target_pairs={{0,8},{8,0},{4,12},{12,4},{1,9},{9,1},{5,13},{13,5},{2,10},{10,2},... | collective-permute-start | bytes 1179656 | tf_op jit(solution)/shard_map/ppermute | solution.py:112
  250.5 25.4 %collective-permute-start.79 = (bf16[256,768]{1,0:T(8,128)(2,1)S(1)}, bf16[256,768]{1,0:T(8,128)(2,1)S(1)}, u32[]{:S(2)}, u32[]{:S(2)}) collective-permute-start(bf16[256,768]{1,0:T(8,128)(2,1)S(1)} %get-tuple-element.102), channel_id=1, source_target_pairs={{0,4},{4,0},{8,12},{12,8},{1,5},{5,1},{9,13},{13,9},{2,6},{6,2},{1... | collective-permute-start | bytes 1179656 | tf_op jit(solution)/shard_map/ppermute | solution.py:108
  318.2 60.3 %collective-permute-start.22 = (bf16[256,768]{1,0:T(8,128)(2,1)}, bf16[256,768]{1,0:T(8,128)(2,1)}, u32[]{:S(2)}, u32[]{:S(2)}) collective-permute-start(bf16[256,768]{1,0:T(8,128)(2,1)} %get-tuple-element.104), channel_id=1, source_target_pairs={{0,4},{4,0},{8,12},{12,8},{1,5},{5,1},{9,13},{13,9},{2,6},{6,2},{1... | collective-permute-start | bytes 1179656 | tf_op jit(solution)/shard_map/ppermute | solution.py:108
  319.5 60.4 %collective-permute-start.20 = (bf16[256,768]{1,0:T(8,128)(2,1)}, bf16[256,768]{1,0:T(8,128)(2,1)}, u32[]{:S(2)}, u32[]{:S(2)}) collective-permute-start(bf16[256,768]{1,0:T(8,128)(2,1)} %get-tuple-element.103), channel_id=1, source_target_pairs={{0,8},{8,0},{4,12},{12,4},{1,9},{9,1},{5,13},{13,5},{2,10},{10,2},... | collective-permute-start | bytes 1179656 | tf_op jit(solution)/shard_map/ppermute | solution.py:112
  321.0 58.8 %collective-permute-start.24 = (bf16[256,768]{1,0:T(8,128)(2,1)}, bf16[256,768]{1,0:T(8,128)(2,1)}, u32[]{:S(2)}, u32[]{:S(2)}) collective-permute-start(bf16[256,768]{1,0:T(8,128)(2,1)} %collective-permute-done.23), channel_id=1, source_target_pairs={{0,4},{4,0},{8,12},{12,8},{1,5},{5,1},{9,13},{13,9},{2,6},{6,2},{1... | collective-permute-start | bytes 1179656 | tf_op jit(solution)/shard_map/ppermute | solution.py:108
  321.8 58.0 %collective-permute-start.21 = (bf16[256,768]{1,0:T(8,128)(2,1)}, bf16[256,768]{1,0:T(8,128)(2,1)}, u32[]{:S(2)}, u32[]{:S(2)}) collective-permute-start(bf16[256,768]{1,0:T(8,128)(2,1)} %collective-permute-done.19), channel_id=1, source_target_pairs={{0,8},{8,0},{4,12},{12,4},{1,9},{9,1},{5,13},{13,5},{2,10},{10,2},... | collective-permute-start | bytes 1179656 | tf_op jit(solution)/shard_map/ppermute | solution.py:112
  322.3 143.6 %collective-permute-start.45 = (bf16[512,384]{1,0:T(8,128)(2,1)}, bf16[512,384]{1,0:T(8,128)(2,1)}, u32[]{:S(2)}, u32[]{:S(2)}) collective-permute-start(bf16[512,384]{1,0:T(8,128)(2,1)} %slice.339), channel_id=1, source_target_pairs={{0,1},{1,2},{2,3},{3,0},{4,5},{5,6},{6,7},{7,4},{8,9},{9,10},{10,1... | collective-permute-start | bytes 1179656 | tf_op jit(solution)/shard_map/ppermute | solution.py:142
  378.5 65.7 %collective-permute-start.64 = (f32[2,512]{1,0:T(2,128)}, f32[2,512]{1,0:T(2,128)}, u32[]{:S(2)}, u32[]{:S(2)}) collective-permute-start(f32[2,512]{1,0:T(2,128)} %pad_maximum_fusion.12), channel_id=1, source_target_pairs={{0,4},{4,0},{8,12},{12,8},{1,5},{5,1},{9,13},{13,9},{2,6},{6,2},{1... | collective-permute-start | bytes 12296 | tf_op jit(solution)/shard_map/ppermute | solution.py:108
  379.8 178.7 %collective-permute-start.90 = (bf16[1536,1536]{1,0:T(8,128)(2,1)}, bf16[1536,1536]{1,0:T(8,128)(2,1)}, u32[]{:S(2)}, u32[]{:S(2)}) collective-permute-start(bf16[1536,1536]{1,0:T(8,128)(2,1)} %convolution_convert_fusion), channel_id=1, source_target_pairs={{0,16},{16,0},{1,17},{17,1},{2,18},{18,2},{3,19},{19,3},{4,20},{20... | collective-permute-start | bytes 14155784 | tf_op jit(solution)/shard_map/ppermute | solution.py:116
  461.7 30.8 %collective-permute-start.25 = (bf16[512,384]{1,0:T(8,128)(2,1)S(1)}, bf16[512,384]{1,0:T(8,128)(2,1)S(1)}, u32[]{:S(2)}, u32[]{:S(2)}) collective-permute-start(bf16[512,384]{1,0:T(8,128)(2,1)S(1)} %slice.323), channel_id=1, source_target_pairs={{0,1},{1,2},{2,3},{3,0},{4,5},{5,6},{6,7},{7,4},{8,9},{9,10},{10,1... | collective-permute-start | bytes 1179656 | tf_op jit(solution)/shard_map/ppermute | solution.py:142
  465.8 26.6 %collective-permute-start.61 = (bf16[512,384]{1,0:T(8,128)(2,1)S(1)}, bf16[512,384]{1,0:T(8,128)(2,1)S(1)}, u32[]{:S(2)}, u32[]{:S(2)}) collective-permute-start(bf16[512,384]{1,0:T(8,128)(2,1)S(1)} %slice.353), channel_id=1, source_target_pairs={{0,1},{1,2},{2,3},{3,0},{4,5},{5,6},{6,7},{7,4},{8,9},{9,10},{10,1... | collective-permute-start | bytes 1179656 | tf_op jit(solution)/shard_map/ppermute | solution.py:142
  465.9 104.3 %collective-permute-start.91 = (bf16[3072,768]{1,0:T(8,128)(2,1)}, bf16[3072,768]{1,0:T(8,128)(2,1)}, u32[]{:S(2)}, u32[]{:S(2)}) collective-permute-start(bf16[3072,768]{1,0:T(8,128)(2,1)} %convolution_convert_fusion.1), channel_id=1, source_target_pairs={{0,16},{16,0},{1,17},{17,1},{2,18},{18,2},{3,19},{19,3},{4,20},{20... | collective-permute-start | bytes 14155784 | tf_op jit(solution)/shard_map/ppermute | solution.py:116
  484.0 33.8 %collective-permute-start.46 = (bf16[512,384]{1,0:T(8,128)(2,1)S(1)}, bf16[512,384]{1,0:T(8,128)(2,1)S(1)}, u32[]{:S(2)}, u32[]{:S(2)}) collective-permute-start(bf16[512,384]{1,0:T(8,128)(2,1)S(1)} %add_convert_fusion.10), channel_id=1, source_target_pairs={{0,1},{1,2},{2,3},{3,0},{4,5},{5,6},{6,7},{7,4},{8,9},{9,10},{10,1... | collective-permute-start | bytes 1179656 | tf_op jit(solution)/shard_map/ppermute | solution.py:142
  (152 other events, 2304.5 us)

commit v2 on v1

--- a/solution.py
+++ b/solution.py
@@ -5,7 +5,6 @@
 
 D = 6144
 CHUNKS = 2
-LAG = 2
 
 
 EPSILON = 1e-06
@@ -95,8 +94,11 @@
     return lax.dynamic_slice_in_dim(values, index * width, width, axis)
 
 
-def reorder(values, axis, order, width):
-    return jnp.concatenate([take_block(values, axis, index, width) for index in order], axis=axis)
+def place(rows, width, pieces):
+    whole = jnp.zeros((rows, 4 * width), pieces[0][0].dtype)
+    for values, at, index in pieces:
+        whole = lax.dynamic_update_slice(whole, values, (at, index * width))
+    return whole
 
 
 RING_UP = [(0, 1), (1, 2), (2, 3), (3, 0)]
@@ -127,42 +129,45 @@
     )
 
 
-def gather_col(values):
+def gather_col(values, owners):
     pieces = [values]
     for _ in range(3):
         pieces.append(lax.ppermute(pieces[-1], "col", RING_DOWN))
-    return pieces
-
-
-def scatter_col(partial):
+    rows, width = values.shape
+    return place(rows, width, [(p, 0, o) for p, o in zip(pieces, owners)]), pieces
+
+
+def scatter_col(partial, owners):
     width = partial.shape[1] // 4
-    block = lambda j: partial[:, j * width:(j + 1) * width]
-    moving = block(3)
+    block = lambda j: take_block(partial, 1, owners[j], width)
+    moving, arrived = block(3), []
     for j in (2, 1, 0):
-        moving = block(j).astype(jnp.float32) + lax.ppermute(moving, "col", RING_UP).astype(jnp.float32)
+        arrived.append(lax.ppermute(moving, "col", RING_UP))
+        moving = block(j).astype(jnp.float32) + arrived[-1].astype(jnp.float32)
         if j:
             moving = moving.astype(jnp.bfloat16)
-    return moving
-
-
-def gather_row(values):
-    half = values.shape[0] // 2
+    return moving, arrived
+
+
+def gather_row(values, owners):
+    rows, width = values.shape
+    half = rows // 2
     top, low = values[:half], values[half:]
     top_x, low_y = over_x(top), over_y(low)
     top_y, low_x = over_y(top), over_x(low)
-    return jnp.concatenate(
-        [
-            jnp.concatenate([top, top_x, top_y, over_y(top_x)], axis=1),
-            jnp.concatenate([low, low_x, low_y, over_x(low_y)], axis=1),
-        ],
-        axis=0,
-    )
-
-
-def scatter_row(partial):
+    upper = [top, top_x, top_y, over_y(top_x)]
+    lower = [low, low_x, low_y, over_x(low_y)]
+    return place(
+        rows,
+        width,
+        [(p, 0, o) for p, o in zip(upper, owners)] + [(p, half, o) for p, o in zip(lower, owners)],
+    ), upper
+
+
+def scatter_row(partial, owners):
     half, width = partial.shape[0] // 2, partial.shape[1] // 4
-    top = lambda j: partial[:half, j * width:(j + 1) * width]
-    low = lambda j: partial[half:, j * width:(j + 1) * width]
+    top = lambda j: take_block(partial[:half], 1, owners[j], width)
+    low = lambda j: take_block(partial[half:], 1, owners[j], width)
     wide = lambda values: values.astype(jnp.float32)
     top_far, low_far = over_x(top(3)), over_y(low(3))
     top_near, low_near = over_x(top(1)), over_y(low(2))
@@ -177,6 +182,9 @@
     )
 
 
+fixed = lax.optimization_barrier
+
+
 def after(values, earlier):
     return lax.optimization_barrier((values, earlier))[0]
 
@@ -186,7 +194,6 @@
     row, col, core = lax.axis_index("row"), lax.axis_index("col"), lax.axis_index("depth")
     hidden = up_weight.shape[1] // 4
     turned = [lax.rem(col + j, 4) for j in range(4)]
-    turned_back = [lax.rem(j - col + 4, 4) for j in range(4)]
     flipped = [row ^ j for j in range(4)]
 
     local = activations.astype(jnp.float32)
@@ -194,81 +201,87 @@
         jnp.stack([jnp.sum(local, axis=1), jnp.sum(local * local, axis=1)], axis=0)
     )
     gain_local = norm_gain.astype(jnp.float32).reshape(1, shard)
-    gain_block = jnp.concatenate(gather_col(gain_local), axis=1)
+    gain_block = gather_col(gain_local, turned)[0]
     centre = (sums[0] / D)[:, None]
     spread = lax.rsqrt(sums[1][:, None] / D - centre * centre + EPSILON)
 
-    up = reorder(reorder(up_weight, 0, turned, shard), 1, flipped, hidden)
-    down = reorder(reorder(down_weight, 1, turned, shard), 0, flipped, hidden)
+    up, down = up_weight, down_weight
 
     size = tokens // CHUNKS
     parts = [slice(k * size, (k + 1) * size) for k in range(CHUNKS)]
     behind = None
     grad_rows, raw = [], []
     for part in parts:
-        for source, store in ((upstream, grad_rows), (activations, raw)):
+        for source, store, lag in ((upstream, grad_rows, 1), (activations, raw, 3)):
             piece = source[part]
             if behind is not None:
                 piece = after(piece, behind)
-            pieces = gather_col(piece)
-            behind = pieces[LAG]
-            store.append(jnp.concatenate(pieces, axis=1))
+            whole, pieces = gather_col(piece, turned)
+            behind = pieces[lag]
+            store.append(fixed(whole))
 
     whitened, normed, activated, gated, branch, grad_normed, sums_back = ([] for _ in range(7))
+    marks = []
+    down_sent, down_kept = [], []
+
+    def half_product(left, right, half_at):
+        return inner_rows(left, take_block(right, 1, half_at, right.shape[1] // 2))
+
     for k, part in enumerate(parts):
-        grad_pre = scatter_row(inner_cols(grad_rows[k], down).astype(jnp.bfloat16))
+        partial_hidden = inner_cols(grad_rows[k], down).astype(jnp.bfloat16)
+        if marks:
+            partial_hidden = after(partial_hidden, marks[0])
+        grad_pre = scatter_row(partial_hidden, flipped)
         whitened.append((raw[k].astype(jnp.float32) - centre[part]) * spread[part])
-        normed.append((whitened[k] * gain_block).astype(jnp.bfloat16))
-        pre_act = scatter_row(
-            jnp.dot(normed[k], up, preferred_element_type=jnp.float32).astype(jnp.bfloat16)
+        normed.append(fixed((whitened[k] * gain_block).astype(jnp.bfloat16)))
+        partial_up = jnp.dot(normed[k], up, preferred_element_type=jnp.float32).astype(jnp.bfloat16)
+        if marks:
+            partial_up = after(partial_up, marks[1])
+        pre_act = scatter_row(partial_up, flipped)
+        own_activated = fixed(gelu_value(pre_act).astype(jnp.bfloat16))
+        if marks:
+            own_activated = after(own_activated, marks[2])
+        whole, _ = gather_row(own_activated, flipped)
+        activated.append(fixed(whole))
+        own_gated = fixed((grad_pre * gelu_slope(pre_act)).astype(jnp.bfloat16))
+        if marks:
+            own_gated = after(own_gated, marks[3])
+        whole, hops = gather_row(own_gated, flipped)
+        gated.append(fixed(whole))
+        summed, branch_steps = scatter_col(
+            jnp.dot(activated[k], down, preferred_element_type=jnp.float32).astype(jnp.bfloat16),
+            turned,
         )
-        activated.append(gather_row(gelu_value(pre_act).astype(jnp.bfloat16)))
-        gated.append(gather_row((grad_pre * gelu_slope(pre_act)).astype(jnp.bfloat16)))
-        branch.append(
-            scatter_col(
-                jnp.dot(activated[k], down, preferred_element_type=jnp.float32).astype(jnp.bfloat16)
-            ).astype(jnp.bfloat16)
-        )
+        branch.append(summed.astype(jnp.bfloat16))
+        down_sent.append(half_product(activated[k], grad_rows[k], 1 - core))
+        down_kept.append(half_product(activated[k], grad_rows[k], core))
         partial = inner_cols(gated[k], up).astype(jnp.bfloat16)
         wide = partial.astype(jnp.float32) * gain_block
         sums_back.append(
-            total_over_slice(
-                jnp.stack([jnp.sum(wide, axis=1), jnp.sum(wide * whitened[k], axis=1)], axis=0)
-            )
+            jnp.stack([jnp.sum(wide, axis=1), jnp.sum(wide * whitened[k], axis=1)], axis=0)
         )
-        grad_normed.append(scatter_col(partial))
-
-    def over_tokens(blocks, axis_order, width):
-        return jnp.concatenate([reorder(block, 1, axis_order, width) for block in blocks], axis=0)
-
-    def split(order):
-        keep = [jnp.where(core == 0, order[b], order[2 + b]) for b in range(2)]
-        send = [jnp.where(core == 0, order[2 + b], order[b]) for b in range(2)]
-        return keep, send
-
-    hidden_keep, hidden_send = split(flipped)
-    width_keep, width_send = split(turned_back)
-
-    whole_activated = over_tokens(activated, flipped, hidden)
-    down_send = inner_rows(whole_activated, over_tokens(grad_rows, width_send, shard))
-    down_got = over_core(down_send.astype(jnp.bfloat16))
-    grad_down = inner_rows(
-        whole_activated, over_tokens(grad_rows, width_keep, shard)
-    ) + down_got.astype(jnp.float32)
-
-    whole_normed = over_tokens(normed, turned_back, shard)
-    up_send = inner_rows(whole_normed, over_tokens(gated, hidden_send, hidden))
-    up_got = over_core(up_send.astype(jnp.bfloat16))
-    grad_up = inner_rows(
-        whole_normed, over_tokens(gated, hidden_keep, hidden)
-    ) + up_got.astype(jnp.float32)
+        summed, back_steps = scatter_col(partial, turned)
+        grad_normed.append(summed)
+        marks = [hops[1], branch_steps[0], (branch_steps[2], back_steps[0]), back_steps[1]]
+
+    totals_back = total_over_slice(jnp.concatenate(sums_back, axis=1))
+
+    down_got = over_core(sum(down_sent).astype(jnp.bfloat16))
+    grad_down = sum(down_kept) + down_got.astype(jnp.float32)
+    late = [after(b, back_steps[0]) for b in gated]
+    later = [after(b, back_steps[1]) for b in gated]
+    up_sent = sum(half_product(a, b, 1 - core) for a, b in zip(normed, late))
+    up_got = over_core(up_sent.astype(jnp.bfloat16))
+    grad_up = sum(half_product(a, b, core) for a, b in zip(normed, later)) + up_got.astype(
+        jnp.float32
+    )
 
     grad_input, gain_part = [], 0.0
     for k, part in enumerate(parts):
         white = (local[part] - centre[part]) * spread[part]
         scaled = grad_normed[k] * gain_local
-        mean_grad = (sums_back[k][0] / D)[:, None]
-        mean_cross = (sums_back[k][1] / D)[:, None]
+        mean_grad = (totals_back[0][part] / D)[:, None]
+        mean_cross = (totals_back[1][part] / D)[:, None]
         grad_input.append(
             (spread[part] * (scaled - mean_grad - white * mean_cross)).astype(jnp.bfloat16)
         )

time: 627 us -> 486 us (0.78)
  matrix products: 193 us -> 111 us
  other arithmetic: 68.4 us -> 32.9 us
  local copies, waits for them, and re-layouts: 52 us -> 23.3 us
    dot_general x4 -> x8, matrix products: 111 us -> 46.6 us  [inner_rows(): lax.dot_general(left, right, (((0,), (0,)), ((), ())), preferred_element_...]
    concatenate x8 -> x1, other arithmetic: 41.8 us -> 0.01 us  [body(): totals_back = total_over_slice(jnp.concatenate(sums_back, axis=1))]
    dynamic_slice x12, local copies, waits for them, and re-layouts: 34.1 us -> 4.08 us  [take_block(): return lax.dynamic_slice_in_dim(values, index * width, width, axis)]
    ppermute x12, waiting for transfers between devices: 83.4 us -> 58.6 us  [scatter_col(): arrived.append(lax.ppermute(moving, 'col', RING_UP))]
    ppermute x27 -> x26, waiting for transfers between devices: 29.8 us -> 52.3 us  [over_x(): return lax.ppermute(values, 'row', [(0, 1), (1, 0), (2, 3), (3, 2)])]
    add x0 -> x1, other arithmetic: none -> 12.4 us  [body(): grad_down = sum(down_kept) + down_got.astype(jnp.float32)]
    ppermute x15, waiting for transfers between devices: 30.7 us -> 42.8 us  [gather_col(): pieces.append(lax.ppermute(pieces[-1], 'col', RING_DOWN))]
    ppermute x15, starting transfers between devices: 38.7 us -> 50.3 us  [gather_col(): pieces.append(lax.ppermute(pieces[-1], 'col', RING_DOWN))]
  transfers between devices with their start and end apart: 93 -> 88, of which waited for: 41 -> 39; matrix products, arithmetic and copies ran while one was open for 42% -> 31% of each run, Pallas kernels for 0% -> 0%
where the time goes in v2:
time: 486 us; the launch traced here: 479 us
  waiting for transfers between devices  196 us (40%)
  starting transfers between devices  113 us (23%)
  matrix products  111 us (23%)
  other arithmetic  32.9 us (7%)
  local copies, waits for them, and re-layouts  23.3 us (5%)
    ppermute x12, waiting for transfers between devices, scatter_col(): arrived.append(lax.ppermute(moving, 'col', RING_UP))  58.6 us
    ppermute x26, waiting for transfers between devices, over_x(): return lax.ppermute(values, 'row', [(0, 1), (1, 0), (2, 3), (3, 2)])  52.3 us
    ppermute x15, starting transfers between devices, gather_col(): pieces.append(lax.ppermute(pieces[-1], 'col', RING_DOWN))  50.3 us
    dot_general x8, matrix products, inner_rows(): lax.dot_general(left, right, (((0,), (0,)), ((), ())), preferred_element_...  46.6 us
    ppermute x15, waiting for transfers between devices, gather_col(): pieces.append(lax.ppermute(pieces[-1], 'col', RING_DOWN))  42.8 us
    ppermute x26, waiting for transfers between devices, over_y(): return lax.ppermute(values, 'row', [(0, 2), (2, 0), (1, 3), (3, 1)])  42.5 us
    dot_general x4, matrix products, inner_cols(): lax.dot_general(left, right, (((1,), (1,)), ((), ())), preferred_element_...  35.2 us
    ppermute x26, starting transfers between devices, over_x(): return lax.ppermute(values, 'row', [(0, 1), (1, 0), (2, 3), (3, 2)])  26.5 us
  transfers between devices with their start and end apart: 88, of which 39 were waited for; matrix products, arithmetic and copies ran while one was open for 31% of the time, Pallas kernels for 0%

profile of v2, /device:TPU:0, one launch (start us, length us, event | category | flops | bytes accessed | tf_op | source)
XLA Modules:
  0.0 479.0 jit_solution(14474705023466175557)
XLA Ops:
  35.3 9.8 %collective-permute-done.37 = bf16[512,384]{1,0:T(8,128)(2,1)S(1)} collective-permute-done((bf16[512,384]{1,0:T(8,128)(2,1)}, bf16[512,384]{1,0:T(8,128)(2,1)S(1)}, u32[]{:S(2)}, u32[]{:S(2)}) %collective-permute-start.37) | collective-permute-done | bytes 393248 | tf_op jit(solution)/shard_map/ppermute | solution.py:135
  61.1 9.1 %convolution_convert_fusion.1 = bf16[512,3072]{1,0:T(8,128)(2,1)S(1)} fusion(bf16[512,1536]{1,0:T(8,128)(2,1)S(1)} %constant_dynamic-update-slice_fusion.16, bf16[3072,1536]{1,0:T(8,128)(2,1)} %param.8), kind=kOutput, calls=%fused_computation.5 | convolution fusion | flops 4833411072 | bytes 14155776 | tf_op jit(solution)/shard_map/dot_general | solution.py:32
  76.5 5.9 %collective-permute-done.3 = bf16[512,384]{1,0:T(8,128)(2,1)S(1)} collective-permute-done((bf16[512,384]{1,0:T(8,128)(2,1)S(1)}, bf16[512,384]{1,0:T(8,128)(2,1)S(1)}, u32[]{:S(2)}, u32[]{:S(2)}) %collective-permute-start.3) | collective-permute-done | bytes 393248 | tf_op jit(solution)/shard_map/ppermute | solution.py:135
  100.3 7.1 %collective-permute-done.28 = bf16[512,384]{1,0:T(8,128)(2,1)S(1)} collective-permute-done((bf16[512,384]{1,0:T(8,128)(2,1)S(1)}, bf16[512,384]{1,0:T(8,128)(2,1)S(1)}, u32[]{:S(2)}, u32[]{:S(2)}) %collective-permute-start.28) | collective-permute-done | bytes 393248 | tf_op jit(solution)/shard_map/ppermute | solution.py:135
  112.2 9.0 %collective-permute-done.29 = bf16[512,384]{1,0:T(8,128)(2,1)S(1)} collective-permute-done((bf16[512,384]{1,0:T(8,128)(2,1)S(1)}, bf16[512,384]{1,0:T(8,128)(2,1)S(1)}, u32[]{:S(2)}, u32[]{:S(2)}) %collective-permute-start.29) | collective-permute-done | bytes 393248 | tf_op jit(solution)/shard_map/ppermute | solution.py:135
  131.9 9.9 %convolution_convert_fusion.3 = bf16[512,3072]{1,0:T(8,128)(2,1)S(1)} fusion(bf16[512,1536]{1,0:T(8,128)(2,1)S(1)} %get-tuple-element.88, bf16[1536,3072]{1,0:T(8,128)(2,1)} %param.7), kind=kOutput, calls=%fused_computation.7 | convolution fusion | flops 4833411072 | bytes 14155776 | tf_op jit(solution)/shard_map/dot_general | solution.py:237
  153.9 6.4 %convolution_convert_fusion = bf16[512,3072]{1,0:T(8,128)(2,1)} fusion(bf16[512,1536]{1,0:T(8,128)(2,1)S(1)} %constant_dynamic-update-slice_fusion.4, bf16[3072,1536]{1,0:T(8,128)(2,1)S(1)} %bitcast.79), kind=kOutput, calls=%fused_computation.4 | convolution fusion | flops 4833411072 | bytes 14155776 | tf_op jit(solution)/shard_map/dot_general | solution.py:32
  160.3 7.8 %collective-permute-done.17 = bf16[256,768]{1,0:T(8,128)(2,1)S(1)} collective-permute-done((bf16[256,768]{1,0:T(8,128)(2,1)S(1)}, bf16[256,768]{1,0:T(8,128)(2,1)S(1)}, u32[]{:S(2)}, u32[]{:S(2)}) %collective-permute-start.17) | collective-permute-done | bytes 393248 | tf_op jit(solution)/shard_map/ppermute | solution.py:110
  169.8 9.4 %convolution_convert_fusion.2 = bf16[512,3072]{1,0:T(8,128)(2,1)S(1)} fusion(bf16[512,1536]{1,0:T(8,128)(2,1)S(1)} %get-tuple-element.89, bf16[1536,3072]{1,0:T(8,128)(2,1)} %param.7), kind=kOutput, calls=%fused_computation.6 | convolution fusion | flops 4833411072 | bytes 14155776 | tf_op jit(solution)/shard_map/dot_general | solution.py:237
  195.4 11.3 %collective-permute-done.46 = bf16[256,768]{1,0:T(8,128)(2,1)S(1)} collective-permute-done((bf16[256,768]{1,0:T(8,128)(2,1)S(1)}, bf16[256,768]{1,0:T(8,128)(2,1)S(1)}, u32[]{:S(2)}, u32[]{:S(2)}) %collective-permute-start.46) | collective-permute-done | bytes 393248 | tf_op jit(solution)/shard_map/ppermute | solution.py:114
  212.3 10.7 %collective-permute-done.23 = bf16[256,768]{1,0:T(8,128)(2,1)S(1)} collective-permute-done((bf16[256,768]{1,0:T(8,128)(2,1)S(1)}, bf16[256,768]{1,0:T(8,128)(2,1)S(1)}, u32[]{:S(2)}, u32[]{:S(2)}) %collective-permute-start.23) | collective-permute-done | bytes 393248 | tf_op jit(solution)/shard_map/ppermute | solution.py:110
  248.4 7.9 %convolution_convert_fusion.6 = bf16[512,1536]{1,0:T(8,128)(2,1)S(1)} fusion(bf16[512,3072]{1,0:T(8,128)(2,1)S(1)} %constant_dynamic-update-slice_fusion.40, bf16[1536,3072]{1,0:T(8,128)(2,1)} %param.7), kind=kOutput, calls=%fused_computation.20 | convolution fusion | flops 4832624640 | bytes 14155776 | tf_op jit(solution)/shard_map/dot_general | solution.py:32
  263.8 12.4 %collective-permute-done.51 = bf16[512,384]{1,0:T(8,128)(2,1)S(1)} collective-permute-done((bf16[512,384]{1,0:T(8,128)(2,1)S(1)}, bf16[512,384]{1,0:T(8,128)(2,1)S(1)}, u32[]{:S(2)}, u32[]{:S(2)}) %collective-permute-start.51) | collective-permute-done | bytes 393248 | tf_op jit(solution)/shard_map/ppermute | solution.py:145
  290.7 6.9 %collective-permute-done.25 = bf16[512,384]{1,0:T(8,128)(2,1)S(1)} collective-permute-done((bf16[512,384]{1,0:T(8,128)(2,1)S(1)}, bf16[512,384]{1,0:T(8,128)(2,1)S(1)}, u32[]{:S(2)}, u32[]{:S(2)}) %collective-permute-start.25) | collective-permute-done | bytes 393248 | tf_op jit(solution)/shard_map/ppermute | solution.py:145
  303.7 6.0 %collective-permute-done.33 = bf16[256,768]{1,0:T(8,128)(2,1)S(1)} collective-permute-done((bf16[256,768]{1,0:T(8,128)(2,1)S(1)}, bf16[256,768]{1,0:T(8,128)(2,1)S(1)}, u32[]{:S(2)}, u32[]{:S(2)}) %collective-permute-start.33) | collective-permute-done | bytes 393248 | tf_op jit(solution)/shard_map/ppermute | solution.py:114
  357.0 11.7 %fusion.1 = (f32[512]{0:T(512)S(1)}, f32[512]{0:T(512)S(1)}, f32[512]{0:T(512)S(1)}, f32[512]{0:T(512)S(1)}, bf16[512,1536]{1,0:T(8,128)(2,1)}) fusion(bf16[512,1536]{1,0:T(8,128)(2,1)} %copy-done.5, f32[1536]{0:T(1024)S(1)} %dynamic_update_slice.167, f32[512]{0:T(512)S(1)} %bitcast.48, f32[512]{0:T(512)S(1)} %bitcast.54, ...), kind=kOutput, calls=%fused_computation.13 | convolution fusion | flops 4845205504 | bytes 18896896 | tf_op jit(solution)/shard_map/dot_general | solution.py:32
  371.4 6.3 %fusion.20 = f32[3072,768]{1,0:T(8,128)} fusion(bf16[512,3072]{1,0:T(8,128)(2,1)S(1)} %get-tuple-element.100, bf16[512,1536]{1,0:T(8,128)(2,1)} %copy-done.3, s32[]{:T(128)S(6)} %select_n.39), kind=kOutput, calls=%fused_computation.55 | convolution fusion | flops 2415919104 | bytes 13369348 | tf_op jit(solution)/shard_map/dot_general | solution.py:26
  378.5 6.7 %add_convert_fusion = bf16[3072,768]{1,0:T(8,128)(2,1)} fusion(f32[3072,768]{1,0:T(8,128)} %fusion.20, bf16[512,3072]{1,0:T(8,128)(2,1)S(1)} %constant_dynamic-update-slice_fusion.44, bf16[512,1536]{1,0:T(8,128)(2,1)S(1)} %constant_dynamic-update-slice_fusion.16, s32[]{:T(128)S(6)} %select_n.39), kind=kOutput, calls=%fused_computation.1 | convolution fusion | flops 2420637696 | bytes 18087940 | tf_op jit(solution)/shard_map/dot_general | solution.py:26
  390.2 6.6 %fusion.12 = f32[1536,1536]{1,0:T(8,128)} fusion(bf16[512,1536]{1,0:T(8,128)(2,1)S(1)} %copy-done.9, bf16[512,3072]{1,0:T(8,128)(2,1)} %get-tuple-element.24, s32[]{:T(128)S(6)} %select_n.37), kind=kOutput, calls=%fused_computation.36 | convolution fusion | flops 2415919104 | bytes 12582916 | tf_op jit(solution)/shard_map/dot_general | solution.py:26
  396.8 6.9 %add_convert_fusion.1 = bf16[1536,1536]{1,0:T(8,128)(2,1)} fusion(f32[1536,1536]{1,0:T(8,128)} %fusion.12, bf16[512,1536]{1,0:T(8,128)(2,1)S(1)} %get-tuple-element.88, bf16[512,3072]{1,0:T(8,128)(2,1)S(1)} %constant_dynamic-update-slice_fusion.40, s32[]{:T(128)S(6)} %select_n.37), kind=kOutput, calls=%fused_computation.3 | convolution fusion | flops 2420637696 | bytes 17301508 | tf_op jit(solution)/shard_map/dot_general | solution.py:26
  414.1 17.0 %collective-permute-done.59 = bf16[512,384]{1,0:T(8,128)(2,1)S(1)} collective-permute-done((bf16[512,384]{1,0:T(8,128)(2,1)S(1)}, bf16[512,384]{1,0:T(8,128)(2,1)S(1)}, u32[]{:S(2)}, u32[]{:S(2)}) %collective-permute-start.59) | collective-permute-done | bytes 393248 | tf_op jit(solution)/shard_map/ppermute | solution.py:145
  431.3 8.2 %collective-permute-done.83 = bf16[512,384]{1,0:T(8,128)(2,1)S(1)} collective-permute-done((bf16[512,384]{1,0:T(8,128)(2,1)S(1)}, bf16[512,384]{1,0:T(8,128)(2,1)S(1)}, u32[]{:S(2)}, u32[]{:S(2)}) %collective-permute-start.83) | collective-permute-done | bytes 393248 | tf_op jit(solution)/shard_map/ppermute | solution.py:145
  443.9 12.0 %collective-permute-done.84 = bf16[512,384]{1,0:T(8,128)(2,1)S(1)} collective-permute-done((bf16[512,384]{1,0:T(8,128)(2,1)S(1)}, bf16[512,384]{1,0:T(8,128)(2,1)S(1)}, u32[]{:S(2)}, u32[]{:S(2)}) %collective-permute-start.84) | collective-permute-done | bytes 393248 | tf_op jit(solution)/shard_map/ppermute | solution.py:145
  460.5 12.4 %convert_add_fusion = f32[3072,768]{1,0:T(8,128)} fusion(bf16[3072,768]{1,0:T(8,128)(2,1)} %collective-permute-done.86, f32[3072,768]{1,0:T(8,128)} %fusion.25, f32[3072,768]{1,0:T(8,128)} %fusion.23), kind=kLoop, calls=%fused_computation | loop fusion | flops 7077888 | bytes 33030144 | tf_op jit(solution)/shard_map/add | solution.py:270
  (357 shorter events, 259.0 us)
Async XLA Ops:
  7.3 23.7 %collective-permute-start = (bf16[512,384]{1,0:T(8,128)(2,1)}, bf16[512,384]{1,0:T(8,128)(2,1)}, u32[]{:S(2)}, u32[]{:S(2)}) collective-permute-start(bf16[512,384]{1,0:T(8,128)(2,1)} %get-tuple-element.78), channel_id=1, source_target_pairs={{0,3},{1,0},{2,1},{3,2},{4,7},{5,4},{6,5},{7,6},{8,11},{9,8},{10,9... | collective-permute-start | bytes 1179656 | tf_op jit(solution)/shard_map/ppermute | solution.py:135
  74.9 23.0 %collective-permute-start.43 = (bf16[256,768]{1,0:T(8,128)(2,1)S(1)}, bf16[256,768]{1,0:T(8,128)(2,1)S(1)}, u32[]{:S(2)}, u32[]{:S(2)}) collective-permute-start(bf16[256,768]{1,0:T(8,128)(2,1)S(1)} %get-tuple-element.58), channel_id=1, source_target_pairs={{0,8},{8,0},{4,12},{12,4},{1,9},{9,1},{5,13},{13,5},{2,10},{10,2},... | collective-permute-start | bytes 1179656 | tf_op jit(solution)/shard_map/ppermute | solution.py:114
  87.6 24.4 %collective-permute-start.42 = (bf16[256,768]{1,0:T(8,128)(2,1)S(1)}, bf16[256,768]{1,0:T(8,128)(2,1)S(1)}, u32[]{:S(2)}, u32[]{:S(2)}) collective-permute-start(bf16[256,768]{1,0:T(8,128)(2,1)S(1)} %get-tuple-element.57), channel_id=1, source_target_pairs={{0,8},{8,0},{4,12},{12,4},{1,9},{9,1},{5,13},{13,5},{2,10},{10,2},... | collective-permute-start | bytes 1179656 | tf_op jit(solution)/shard_map/ppermute | solution.py:114
  89.2 36.3 %collective-permute-start.39 = (bf16[256,768]{1,0:T(8,128)(2,1)S(1)}, bf16[256,768]{1,0:T(8,128)(2,1)S(1)}, u32[]{:S(2)}, u32[]{:S(2)}) collective-permute-start(bf16[256,768]{1,0:T(8,128)(2,1)S(1)} %get-tuple-element.55), channel_id=1, source_target_pairs={{0,4},{4,0},{8,12},{12,8},{1,5},{5,1},{9,13},{13,9},{2,6},{6,2},{1... | collective-permute-start | bytes 1179656 | tf_op jit(solution)/shard_map/ppermute | solution.py:110
  98.7 26.7 %collective-permute-start.41 = (bf16[256,768]{1,0:T(8,128)(2,1)S(1)}, bf16[256,768]{1,0:T(8,128)(2,1)S(1)}, u32[]{:S(2)}, u32[]{:S(2)}) collective-permute-start(bf16[256,768]{1,0:T(8,128)(2,1)S(1)} %add_convert_fusion.12), channel_id=1, source_target_pairs={{0,8},{8,0},{4,12},{12,4},{1,9},{9,1},{5,13},{13,5},{2,10},{10,2},... | collective-permute-start | bytes 1179656 | tf_op jit(solution)/shard_map/ppermute | solution.py:114
  145.1 23.1 %collective-permute-start.12 = (bf16[256,768]{1,0:T(8,128)(2,1)S(1)}, bf16[256,768]{1,0:T(8,128)(2,1)S(1)}, u32[]{:S(2)}, u32[]{:S(2)}) collective-permute-start(bf16[256,768]{1,0:T(8,128)(2,1)S(1)} %get-tuple-element.63), channel_id=1, source_target_pairs={{0,4},{4,0},{8,12},{12,8},{1,5},{5,1},{9,13},{13,9},{2,6},{6,2},{1... | collective-permute-start | bytes 1179656 | tf_op jit(solution)/shard_map/ppermute | solution.py:110
  182.4 29.2 %collective-permute-start.21 = (bf16[256,768]{1,0:T(8,128)(2,1)S(1)}, bf16[256,768]{1,0:T(8,128)(2,1)S(1)}, u32[]{:S(2)}, u32[]{:S(2)}) collective-permute-start(bf16[256,768]{1,0:T(8,128)(2,1)S(1)} %get-tuple-element.79), channel_id=1, source_target_pairs={{0,4},{4,0},{8,12},{12,8},{1,5},{5,1},{9,13},{13,9},{2,6},{6,2},{1... | collective-permute-start | bytes 1179656 | tf_op jit(solution)/shard_map/ppermute | solution.py:110
  182.5 24.8 %collective-permute-start.22 = (bf16[256,768]{1,0:T(8,128)(2,1)S(1)}, bf16[256,768]{1,0:T(8,128)(2,1)S(1)}, u32[]{:S(2)}, u32[]{:S(2)}) collective-permute-start(bf16[256,768]{1,0:T(8,128)(2,1)S(1)} %get-tuple-element.79), channel_id=1, source_target_pairs={{0,8},{8,0},{4,12},{12,4},{1,9},{9,1},{5,13},{13,5},{2,10},{10,2},... | collective-permute-start | bytes 1179656 | tf_op jit(solution)/shard_map/ppermute | solution.py:114
  184.0 22.8 %collective-permute-start.46 = (bf16[256,768]{1,0:T(8,128)(2,1)S(1)}, bf16[256,768]{1,0:T(8,128)(2,1)S(1)}, u32[]{:S(2)}, u32[]{:S(2)}) collective-permute-start(bf16[256,768]{1,0:T(8,128)(2,1)S(1)} %get-tuple-element.75), channel_id=1, source_target_pairs={{0,8},{8,0},{4,12},{12,4},{1,9},{9,1},{5,13},{13,5},{2,10},{10,2},... | collective-permute-start | bytes 1179656 | tf_op jit(solution)/shard_map/ppermute | solution.py:114
  188.4 53.6 %collective-permute-start.48 = (bf16[256,768]{1,0:T(8,128)(2,1)S(1)}, bf16[256,768]{1,0:T(8,128)(2,1)S(1)}, u32[]{:S(2)}, u32[]{:S(2)}) collective-permute-start(bf16[256,768]{1,0:T(8,128)(2,1)S(1)} %get-tuple-element.73), channel_id=1, source_target_pairs={{0,4},{4,0},{8,12},{12,8},{1,5},{5,1},{9,13},{13,9},{2,6},{6,2},{1... | collective-permute-start | bytes 1179656 | tf_op jit(solution)/shard_map/ppermute | solution.py:110
  206.8 25.9 %collective-permute-start.49 = (bf16[256,768]{1,0:T(8,128)(2,1)S(1)}, bf16[256,768]{1,0:T(8,128)(2,1)S(1)}, u32[]{:S(2)}, u32[]{:S(2)}) collective-permute-start(bf16[256,768]{1,0:T(8,128)(2,1)S(1)} %get-tuple-element.73), channel_id=1, source_target_pairs={{0,8},{8,0},{4,12},{12,4},{1,9},{9,1},{5,13},{13,5},{2,10},{10,2},... | collective-permute-start | bytes 1179656 | tf_op jit(solution)/shard_map/ppermute | solution.py:114
  207.3 26.9 %collective-permute-start.69 = (bf16[256,768]{1,0:T(8,128)(2,1)S(1)}, bf16[256,768]{1,0:T(8,128)(2,1)S(1)}, u32[]{:S(2)}, u32[]{:S(2)}) collective-permute-start(bf16[256,768]{1,0:T(8,128)(2,1)S(1)} %get-tuple-element.52), channel_id=1, source_target_pairs={{0,8},{8,0},{4,12},{12,4},{1,9},{9,1},{5,13},{13,5},{2,10},{10,2},... | collective-permute-start | bytes 1179656 | tf_op jit(solution)/shard_map/ppermute | solution.py:114
  211.6 64.9 %collective-permute-start.68 = (bf16[256,768]{1,0:T(8,128)(2,1)}, bf16[256,768]{1,0:T(8,128)(2,1)}, u32[]{:S(2)}, u32[]{:S(2)}) collective-permute-start(bf16[256,768]{1,0:T(8,128)(2,1)} %get-tuple-element.51), channel_id=1, source_target_pairs={{0,8},{8,0},{4,12},{12,4},{1,9},{9,1},{5,13},{13,5},{2,10},{10,2},... | collective-permute-start | bytes 1179656 | tf_op jit(solution)/shard_map/ppermute | solution.py:114
  232.7 47.2 %collective-permute-start.65 = (bf16[256,768]{1,0:T(8,128)(2,1)S(1)}, bf16[256,768]{1,0:T(8,128)(2,1)}, u32[]{:S(2)}, u32[]{:S(2)}) collective-permute-start(bf16[256,768]{1,0:T(8,128)(2,1)S(1)} %get-tuple-element.49), channel_id=1, source_target_pairs={{0,4},{4,0},{8,12},{12,8},{1,5},{5,1},{9,13},{13,9},{2,6},{6,2},{1... | collective-permute-start | bytes 1179656 | tf_op jit(solution)/shard_map/ppermute | solution.py:110
  239.8 38.8 %collective-permute-start.70 = (bf16[256,768]{1,0:T(8,128)(2,1)}, bf16[256,768]{1,0:T(8,128)(2,1)}, u32[]{:S(2)}, u32[]{:S(2)}) collective-permute-start(bf16[256,768]{1,0:T(8,128)(2,1)} %add_convert_fusion.4), channel_id=1, source_target_pairs={{0,4},{4,0},{8,12},{12,8},{1,5},{5,1},{9,13},{13,9},{2,6},{6,2},{1... | collective-permute-start | bytes 1179656 | tf_op jit(solution)/shard_map/ppermute | solution.py:110
  242.0 40.0 %collective-permute-start.67 = (bf16[256,768]{1,0:T(8,128)(2,1)}, bf16[256,768]{1,0:T(8,128)(2,1)}, u32[]{:S(2)}, u32[]{:S(2)}) collective-permute-start(bf16[256,768]{1,0:T(8,128)(2,1)} %add_convert_fusion.5), channel_id=1, source_target_pairs={{0,8},{8,0},{4,12},{12,4},{1,9},{9,1},{5,13},{13,5},{2,10},{10,2},... | collective-permute-start | bytes 1179656 | tf_op jit(solution)/shard_map/ppermute | solution.py:114
  276.5 22.2 %collective-permute-start.34 = (bf16[256,768]{1,0:T(8,128)(2,1)S(1)}, bf16[256,768]{1,0:T(8,128)(2,1)S(1)}, u32[]{:S(2)}, u32[]{:S(2)}) collective-permute-start(bf16[256,768]{1,0:T(8,128)(2,1)S(1)} %get-tuple-element.61), channel_id=1, source_target_pairs={{0,8},{8,0},{4,12},{12,4},{1,9},{9,1},{5,13},{13,5},{2,10},{10,2},... | collective-permute-start | bytes 1179656 | tf_op jit(solution)/shard_map/ppermute | solution.py:114
  279.9 23.8 %collective-permute-start.31 = (bf16[256,768]{1,0:T(8,128)(2,1)S(1)}, bf16[256,768]{1,0:T(8,128)(2,1)S(1)}, u32[]{:S(2)}, u32[]{:S(2)}) collective-permute-start(bf16[256,768]{1,0:T(8,128)(2,1)S(1)} %get-tuple-element.59), channel_id=1, source_target_pairs={{0,4},{4,0},{8,12},{12,8},{1,5},{5,1},{9,13},{13,9},{2,6},{6,2},{1... | collective-permute-start | bytes 1179656 | tf_op jit(solution)/shard_map/ppermute | solution.py:110
  357.0 52.0 %collective-permute-start.58 = (bf16[512,384]{1,0:T(8,128)(2,1)}, bf16[512,384]{1,0:T(8,128)(2,1)}, u32[]{:S(2)}, u32[]{:S(2)}) collective-permute-start(bf16[512,384]{1,0:T(8,128)(2,1)} %constant_dynamic-slice_fusion.5), channel_id=1, source_target_pairs={{0,1},{1,2},{2,3},{3,0},{4,5},{5,6},{6,7},{7,4},{8,9},{9,10},{10,1... | collective-permute-start | bytes 1179656 | tf_op jit(solution)/shard_map/ppermute | solution.py:145
  385.2 75.4 %collective-permute-start.86 = (bf16[3072,768]{1,0:T(8,128)(2,1)}, bf16[3072,768]{1,0:T(8,128)(2,1)}, u32[]{:S(2)}, u32[]{:S(2)}) collective-permute-start(bf16[3072,768]{1,0:T(8,128)(2,1)} %add_convert_fusion), channel_id=1, source_target_pairs={{0,16},{16,0},{1,17},{17,1},{2,18},{18,2},{3,19},{19,3},{4,20},{20... | collective-permute-start | bytes 14155784 | tf_op jit(solution)/shard_map/ppermute | solution.py:118
  403.7 69.3 %collective-permute-start.85 = (bf16[1536,1536]{1,0:T(8,128)(2,1)}, bf16[1536,1536]{1,0:T(8,128)(2,1)S(1)}, u32[]{:S(2)}, u32[]{:S(2)}) collective-permute-start(bf16[1536,1536]{1,0:T(8,128)(2,1)} %add_convert_fusion.1), channel_id=1, source_target_pairs={{0,16},{16,0},{1,17},{17,1},{2,18},{18,2},{3,19},{19,3},{4,20},{20... | collective-permute-start | bytes 14155784 | tf_op jit(solution)/shard_map/ppermute | solution.py:118
  409.0 34.9 %collective-permute-start.62 = (bf16[512,384]{1,0:T(8,128)(2,1)S(1)}, bf16[512,384]{1,0:T(8,128)(2,1)S(1)}, u32[]{:S(2)}, u32[]{:S(2)}) collective-permute-start(bf16[512,384]{1,0:T(8,128)(2,1)S(1)} %copy-done.15), channel_id=1, source_target_pairs={{0,1},{1,2},{2,3},{3,0},{4,5},{5,6},{6,7},{7,4},{8,9},{9,10},{10,1... | collective-permute-start | bytes 1179656 | tf_op jit(solution)/shard_map/ppermute | solution.py:145
  411.1 28.4 %collective-permute-start.83 = (bf16[512,384]{1,0:T(8,128)(2,1)S(1)}, bf16[512,384]{1,0:T(8,128)(2,1)S(1)}, u32[]{:S(2)}, u32[]{:S(2)}) collective-permute-start(bf16[512,384]{1,0:T(8,128)(2,1)S(1)} %add_convert_fusion.3), channel_id=1, source_target_pairs={{0,1},{1,2},{2,3},{3,0},{4,5},{5,6},{6,7},{7,4},{8,9},{9,10},{10,1... | collective-permute-start | bytes 1179656 | tf_op jit(solution)/shard_map/ppermute | solution.py:145
  431.2 26.7 %collective-permute-start.60 = (bf16[512,384]{1,0:T(8,128)(2,1)S(1)}, bf16[512,384]{1,0:T(8,128)(2,1)S(1)}, u32[]{:S(2)}, u32[]{:S(2)}) collective-permute-start(bf16[512,384]{1,0:T(8,128)(2,1)S(1)} %add_convert_fusion.9), channel_id=1, source_target_pairs={{0,1},{1,2},{2,3},{3,0},{4,5},{5,6},{6,7},{7,4},{8,9},{9,10},{10,1... | collective-permute-start | bytes 1179656 | tf_op jit(solution)/shard_map/ppermute | solution.py:145
  (91 other events, 1300.8 us)
